TPU v7x, 512 devices: a whole 4x4x16 slice. The times are simulated.
512 devices in a mesh: leaf: 32 (over z, core), rows: 16 (over y, x).
Axes of the slice: x: 4, y: 4, z: 16, core: 2. Of those that a mesh axis runs over, the one named last changes fastest.
Arguments:
- loc_rhs: float32 [32, 16, 3, 256, 128], P('leaf', 'rows'), may hold values from -6 to 6
- loc_inv: float32 [32, 16, 3, 256, 256], P('leaf', 'rows'), as said below
- loc_low: float32 [32, 16, 3, 2, 256, 256], P('leaf', 'rows'), may hold values from -0.078125 to 0.078125
- loc_parent: int32 [32, 16, 3], P('leaf', 'rows'), may hold values from 0 to 1
- lvl_rhs: float32 [32, 4, 256, 2, 128], P('leaf', None, 'rows'), may hold values from -6 to 6
- lvl_inv: float32 [32, 4, 2, 256, 256], P('leaf', None, None, 'rows'), as said below
- lvl_low: float32 [32, 3, 2, 2, 256, 256], P('leaf', None, None, None, 'rows'), may hold values from -0.25 to 0.25
- lvl_parent: int32 [32, 3, 2], P('leaf'), may hold values from 0 to 3
Outputs:
- loc_sol: float32 [32, 16, 3, 256, 128], P('leaf', 'rows')
- lvl_sol: float32 [32, 4, 256, 2, 128], P('leaf', None, 'rows')
Inputs may be any that keep to these rules, and one draw needn't show every extreme that they name: `loc_parent`: the level-0 slot, on the same leaf device, of each local supernode's parent. `lvl_parent`: for slot k at level l on leaf device p: a value v below 2 names slot v at level l + 1 on device p, a larger one slot v - 2 on device p XOR 2**l. `loc_inv`: lower triangular. `lvl_inv`: lower triangular.
All inputs are finite; a program needn't handle non-finite values.
Results may differ from a plain program's by a relative error of at most 0.00016.
Values sent between devices are 32-bit elements; how exact they have to be, the bound alone decides.
A program may use at most 64 MiB of HBM per device.

v0:
```python
import jax
import jax.numpy as jnp
from jax import lax
from jax.sharding import PartitionSpec as P

precise = lax.Precision.HIGHEST


def swapped(value, axis, apart):
    mask = 2**apart
    pairs = [(source, source ^ mask) for source in range(lax.axis_size(axis))]
    return lax.ppermute(value, axis, pairs)


def transpose_apply(inv_slab, moved):
    return lax.psum_scatter(
        jnp.einsum("kbc,bkn->ckn", inv_slab, moved, precision=precise),
        "rows",
        scatter_dimension=0,
        tiled=True,
    )


def on_device(loc_rhs, loc_inv, loc_low, loc_parent, lvl_rhs, lvl_inv, lvl_low, lvl_parent):
    rhs_local = loc_rhs[0, 0]
    inv_local = loc_inv[0, 0]
    low_local = loc_low[0, 0]
    level_count = lvl_rhs.shape[1]
    strip_rows = lvl_rhs.shape[2]
    slot_count = lvl_rhs.shape[3]
    rhs_count = lvl_rhs.shape[4]
    solved_local = jnp.einsum("ibc,icn->ibn", inv_local, rhs_local, precision=precise)
    local_pick = (loc_parent[0, 0][:, None] == jnp.arange(slot_count)[None, :]).astype(jnp.float32)
    leaf_contrib = jnp.einsum("ijbc,icn->ijbn", low_local, solved_local, precision=precise)
    arrived = lax.psum_scatter(
        jnp.einsum("ik,ijbn->bkjn", local_pick, leaf_contrib, precision=precise),
        "rows",
        scatter_dimension=0,
        tiled=True,
    )
    above_sum = arrived[:, :, 0]
    pending = arrived[:, :, 1]
    solved_strips = []
    parent_picks = []
    for height in range(level_count):
        moved = lvl_rhs[0, height] - above_sum
        inv_rows = lvl_inv[0, height]
        initial = jnp.zeros((strip_rows, slot_count, rhs_count), jnp.float32)

        def apply_inverse(running, shard_piece, piece_start, inv_rows=inv_rows):
            return jnp.einsum("kbc,ckn->bkn", inv_rows, shard_piece, precision=precise)

        result = apply_inverse(
            initial, lax.all_gather(moved, "rows", axis=0, tiled=True), jnp.int32(0)
        )
        solved_strips.append(result)
        if height + 1 < level_count:
            kind_count = 2 if height + 2 < level_count else 1
            low_used = lvl_low[0, height][:, :kind_count]

            def apply_lower(running, shard_piece, piece_start, low_used=low_used):
                return jnp.einsum("kjbc,ckn->bkjn", low_used, shard_piece, precision=precise)

            initial_low = jnp.zeros((strip_rows, slot_count, kind_count, rhs_count), jnp.float32)
            contrib = apply_lower(
                initial_low, lax.all_gather(result, "rows", axis=0, tiled=True), jnp.int32(0)
            )
            outgoing = jnp.concatenate(
                [(contrib[:, :, 0] + pending)[:, :, None], contrib[:, :, 1:]], axis=2
            )
            parent_pick = (
                lvl_parent[0, height][:, None] == jnp.arange(2 * slot_count)[None, :]
            ).astype(jnp.float32)
            parent_picks.append(parent_pick)
            packed = jnp.einsum("kd,bkjn->bdjn", parent_pick, outgoing, precision=precise)
            received = swapped(packed[:, slot_count:], "leaf", height)
            arrived = packed[:, :slot_count] + received
            above_sum = arrived[:, :, 0]
            if kind_count == 2:
                pending = arrived[:, :, 1]
    top_level = level_count - 1
    current = transpose_apply(lvl_inv[0, top_level], solved_strips[top_level])
    results = [None] * level_count
    results[top_level] = current
    current_parent = current
    for height in range(level_count - 2, -1, -1):
        kind_count = 2 if height + 2 < level_count else 1
        if kind_count == 1:
            shared = current[:, :, None]
        else:
            shared = jnp.stack([current, current_parent], axis=2)
        received = swapped(shared, "leaf", height)
        pooled = jnp.concatenate([shared, received], axis=1)
        above_x = jnp.einsum("kd,bdjn->bkjn", parent_picks[height], pooled, precision=precise)
        low_used = lvl_low[0, height][:, :kind_count]

        def partial_terms(row_start, row_count, low_used=low_used, above_x=above_x):
            return jnp.einsum("kjbc,bkjn->ckn", low_used, above_x, precision=precise)

        summed = lax.psum_scatter(
            partial_terms(jnp.int32(0), strip_rows * lax.axis_size("rows")),
            "rows",
            scatter_dimension=0,
            tiled=True,
        )
        current_new = transpose_apply(lvl_inv[0, height], solved_strips[height] - summed)
        results[height] = current_new
        current = current_new
        current_parent = above_x[:, :, 0]
    full_current, full_parent = (
        lax.all_gather(current, "rows", axis=0, tiled=True),
        lax.all_gather(current_parent, "rows", axis=0, tiled=True),
    )
    parent_x = jnp.einsum("ik,bkn->ibn", local_pick, full_current, precision=precise)
    grand_x = jnp.einsum("ik,bkn->ibn", local_pick, full_parent, precision=precise)
    summed_local = jnp.einsum(
        "ijbc,ijbn->icn", low_local, jnp.stack([parent_x, grand_x], axis=1), precision=precise
    )
    local_x = jnp.einsum("ibc,ibn->icn", inv_local, solved_local - summed_local, precision=precise)
    return (local_x[None, None], jnp.stack(results, axis=0)[None])


def solution(mesh):
    in_specs = (
        P("leaf", "rows", None, None, None),
        P("leaf", "rows", None, None, None),
        P("leaf", "rows", None, None, None, None),
        P("leaf", "rows", None),
        P("leaf", None, "rows", None, None),
        P("leaf", None, None, "rows", None),
        P("leaf", None, None, None, "rows", None),
        P("leaf", None, None),
    )
    out_specs = (P("leaf", "rows", None, None, None), P("leaf", None, "rows", None, None))
    return jax.shard_map(
        on_device, mesh=mesh, in_specs=in_specs, out_specs=out_specs, check_vma=False
    )
```

profile of v0, /device:TPU:1, one launch (start us, length us, event | category | flops | bytes accessed | tf_op | source)
XLA Modules:
  0.0 1069.7 jit_solution(6675751713235342531)
XLA Ops:
  7.2 2.2 fusion.14
  9.4 2.7 fusion.4
  12.1 1.5 copy.56
  13.6 1.1 convolution_bitcast_fusion
  15.0 1.2 reshape.40
  16.5 91.2 %reduce-scatter.14.cloned.1.call-done = f32[16,512]{1,0:T(8,128)} async-done(((f32[256,512]{1,0:T(8,128)}), f32[16,512]{1,0:T(8,128)}) %reduce-scatter.14.cloned.1.call-update) | async-done | bytes 32784
  108.5 17.0 %all_gather.27 = f32[256,2,128]{2,1,0:T(2,128)S(1)} all-gather(f32[16,2,128]{2,1,0:T(2,128)S(1)} %fusion.69), channel_id=1, replica_groups=mesh['leaf'=32,'rows'=16] {'rows'}, dimensions={0}, use_global_device_ids=true | all-gather | bytes 278528 | tf_op jit(solution)/shard_map/all_gather | solution.py:54
  125.7 16.7 %all_gather.28 = f32[256,2,128]{2,0,1:T(8,128)S(1)} all-gather(f32[16,2,128]{2,0,1:T(8,128)S(1)} %convolution_bitcast_fusion.20), channel_id=1, replica_groups=mesh['leaf'=32,'rows'=16] {'rows'}, dimensions={0}, use_global_device_ids=true | all-gather | bytes 278528 | tf_op jit(solution)/shard_map/all_gather | solution.py:66
  143.1 15.1 %collective-permute-start = (f32[16,2,2,128]{3,1,2,0:T(2,128)S(1)}, f32[16,2,2,128]{3,1,2,0:T(2,128)S(1)}, u32[]{:S(2)}, u32[]{:S(2)}) collective-permute-start(f32[16,2,2,128]{3,1,2,0:T(2,128)S(1)} %slice.145), channel_id=1, source_target_pairs={{0,16},{16,0},{32,48},{48,32},{64,80},{80,64},{96,112},{112,96},{1... | collective-permute-start | bytes 98312 | tf_op jit(solution)/shard_map/ppermute | solution.py:12
  158.2 0.8 collective-permute-done
  159.1 17.6 %all_gather.29 = f32[256,2,128]{2,1,0:T(2,128)S(1)} all-gather(f32[16,2,128]{2,1,0:T(2,128)S(1)} %fusion.68), channel_id=1, replica_groups=mesh['leaf'=32,'rows'=16] {'rows'}, dimensions={0}, use_global_device_ids=true | all-gather | bytes 278528 | tf_op jit(solution)/shard_map/all_gather | solution.py:54
  176.9 16.5 %all_gather.30 = f32[256,2,128]{2,0,1:T(8,128)S(1)} all-gather(f32[16,2,128]{2,0,1:T(8,128)S(1)} %convolution_bitcast_fusion.19), channel_id=1, replica_groups=mesh['leaf'=32,'rows'=16] {'rows'}, dimensions={0}, use_global_device_ids=true | all-gather | bytes 278528 | tf_op jit(solution)/shard_map/all_gather | solution.py:66
  194.1 3.2 collective-permute-start.1
  197.3 1.4 collective-permute-done.1
  198.8 17.8 %all_gather.31 = f32[256,2,128]{2,1,0:T(2,128)S(1)} all-gather(f32[16,2,128]{2,1,0:T(2,128)S(1)} %fusion.67), channel_id=1, replica_groups=mesh['leaf'=32,'rows'=16] {'rows'}, dimensions={0}, use_global_device_ids=true | all-gather | bytes 278528 | tf_op jit(solution)/shard_map/all_gather | solution.py:54
  216.8 16.1 %all_gather.32 = f32[256,2,128]{2,0,1:T(8,128)S(1)} all-gather(f32[16,2,128]{2,0,1:T(8,128)S(1)} %convolution_bitcast_fusion.18), channel_id=1, replica_groups=mesh['leaf'=32,'rows'=16] {'rows'}, dimensions={0}, use_global_device_ids=true | all-gather | bytes 278528 | tf_op jit(solution)/shard_map/all_gather | solution.py:66
  233.6 4.2 collective-permute-start.2
  237.8 1.2 collective-permute-done.2
  239.0 17.8 %all_gather.33 = f32[256,2,128]{2,1,0:T(2,128)S(1)} all-gather(f32[16,2,128]{2,1,0:T(2,128)S(1)} %fusion.64), channel_id=1, replica_groups=mesh['leaf'=32,'rows'=16] {'rows'}, dimensions={0}, use_global_device_ids=true | all-gather | bytes 278528 | tf_op jit(solution)/shard_map/all_gather | solution.py:54
  257.4 0.8 copy.66
  258.3 1.3 dynamic-slice
  260.2 139.2 %all-reduce.9.cloned.1.call-done = f32[256,2,128]{2,1,0:T(2,128)} async-done(((f32[256,2,128]{2,1,0:T(2,128)}), f32[256,2,128]{2,1,0:T(2,128)}) %all-reduce.9.cloned.1.call-update) | async-done | bytes 262160
  400.2 4.2 collective-permute-start.3
  404.4 1.2 collective-permute-done.3
  405.8 1.3 convolution_bitcast_fusion.9
  407.2 87.7 %reduce-scatter.8.cloned.1.call-done = f32[16,2,128]{2,0,1:T(8,128)} async-done(((f32[256,2,128]{2,0,1:T(8,128)}), f32[16,2,128]{2,0,1:T(8,128)}) %reduce-scatter.8.cloned.1.call-update) | async-done | bytes 16400 | tf_op jit(solution)/shard_map/reduce_scatter | solution.py:100
  494.9 1.1 convolution_bitcast_fusion.8
  496.1 0.8 copy.69
  497.0 116.7 %all-reduce.11.cloned.1.call-done = f32[256,2,128]{2,1,0:T(2,128)} async-done(((f32[256,2,128]{2,1,0:T(2,128)}), f32[256,2,128]{2,1,0:T(2,128)}) %all-reduce.11.cloned.1.call-update) | async-done | bytes 262160
  614.4 3.4 collective-permute-start.4
  617.8 1.3 collective-permute-done.4
  619.3 1.3 convolution_bitcast_fusion.7
  620.7 87.7 %reduce-scatter.10.cloned.1.call-done = f32[16,2,128]{2,0,1:T(8,128)} async-done(((f32[256,2,128]{2,0,1:T(8,128)}), f32[16,2,128]{2,0,1:T(8,128)}) %reduce-scatter.10.cloned.1.call-update) | async-done | bytes 16400 | tf_op jit(solution)/shard_map/reduce_scatter | solution.py:100
  708.4 1.1 convolution_bitcast_fusion.6
  709.6 0.8 copy.75
  710.5 116.7 %all-reduce.13.cloned.1.call-done = f32[256,2,128]{2,1,0:T(2,128)} async-done(((f32[256,2,128]{2,1,0:T(2,128)}), f32[256,2,128]{2,1,0:T(2,128)}) %all-reduce.13.cloned.1.call-update) | async-done | bytes 262160
  828.0 3.8 collective-permute-start.5
  831.8 0.8 collective-permute-done.5
  832.9 1.3 convolution_bitcast_fusion.5
  834.3 85.0 %reduce-scatter.12.cloned.1.call-done = f32[16,2,128]{2,0,1:T(8,128)} async-done(((f32[256,2,128]{2,0,1:T(8,128)}), f32[16,2,128]{2,0,1:T(8,128)}) %reduce-scatter.12.cloned.1.call-update) | async-done | bytes 16400 | tf_op jit(solution)/shard_map/reduce_scatter | solution.py:100
  919.3 1.1 convolution_bitcast_fusion.4
  920.4 0.8 copy.81
  921.4 17.0 %all-gather = f32[256,2,1,128]{3,1,2,0:T(2,128)S(1)} all-gather(f32[16,2,1,128]{3,1,2,0:T(2,128)S(1)} %slice.158), channel_id=2, replica_groups=mesh['leaf'=32,'rows'=16] {'rows'}, dimensions={0}, use_global_device_ids=true | all-gather | bytes 278528 | tf_op jit(solution)/shard_map/all_gather | solution.py:112
  939.0 99.1 %all-reduce.15.cloned.1.call-done = f32[256,2,128]{2,1,0:T(2,128)} async-done(((f32[256,2,128]{2,1,0:T(2,128)}), f32[256,2,128]{2,1,0:T(2,128)}) %all-reduce.15.cloned.1.call-update) | async-done | bytes 262160
  1040.2 17.2 %all_gather.34 = f32[256,2,128]{2,1,0:T(2,128)S(1)} all-gather(f32[16,2,128]{2,1,0:T(2,128)S(1)} %constant_dynamic-slice_fusion), channel_id=1, replica_groups=mesh['leaf'=32,'rows'=16] {'rows'}, dimensions={0}, use_global_device_ids=true | all-gather | bytes 278528 | tf_op jit(solution)/shard_map/all_gather | solution.py:111
  1058.5 2.6 fusion.10
  1061.1 0.9 convolution_bitcast_fusion.3
  1062.0 0.9 copy.89
  (84 shorter events, 11.8 us)
Async XLA Ops:
  7.2 2.2 copy-start
  7.2 100.5 %reduce-scatter.14.cloned.1.call-start = ((), (), s32[]{:S(2)}) async-start(), calls=%async_computation.7 | async-start | bytes 557056
  12.1 1.5 copy-start.6
  14.7 1.5 copy-start.5
  14.8 93.7 %copy-start.4 = (f32[1,4,16,2,128]{4,3,2,1,0:T(2,128)S(1)}, f32[1,4,16,2,128]{4,3,2,1,0:T(2,128)}, u32[]{:S(2)}) copy-start(f32[1,4,16,2,128]{4,3,2,1,0:T(2,128)} %param.12) | copy-start | bytes 196612
  14.8 110.7 %copy-start.3 = (f32[1,4,2,16,256]{4,3,2,1,0:T(8,128)S(1)}, f32[1,4,2,16,256]{4,3,2,1,0:T(8,128)}, u32[]{:S(2)}) copy-start(f32[1,4,2,16,256]{4,3,2,1,0:T(8,128)} %param.13) | copy-start | bytes 393220
  14.8 127.6 %copy-start.2 = (f32[1,3,2,2,16,256]{5,4,3,2,1,0:T(8,128)S(1)}, f32[1,3,2,2,16,256]{5,4,3,2,1,0:T(8,128)}, u32[]{:S(2)}) copy-start(f32[1,3,2,2,16,256]{5,4,3,2,1,0:T(8,128)} %param.14) | copy-start | bytes 589828
  16.2 383.3 %all-reduce.9.cloned.1.call-start = ((), (), s32[]{:S(2)}) async-start(), calls=%async_computation.8 | async-start | bytes 524288
  143.1 16.0 %collective-permute-start = (f32[16,2,2,128]{3,1,2,0:T(2,128)S(1)}, f32[16,2,2,128]{3,1,2,0:T(2,128)S(1)}, u32[]{:S(2)}, u32[]{:S(2)}) collective-permute-start(f32[16,2,2,128]{3,1,2,0:T(2,128)S(1)} %slice.145), channel_id=1, source_target_pairs={{0,16},{16,0},{32,48},{48,32},{64,80},{80,64},{96,112},{112,96},{1... | collective-permute-start | bytes 98312 | tf_op jit(solution)/shard_map/ppermute | solution.py:12
  194.1 4.7 collective-permute-start.1
  233.6 5.4 collective-permute-start.2
  258.3 236.6 %reduce-scatter.8.cloned.1.call-start = ((), (), s32[]{:S(2)}) async-start(), calls=%async_computation.4 | async-start | bytes 278528 | tf_op jit(solution)/shard_map/reduce_scatter | solution.py:100
  400.2 5.4 collective-permute-start.3
  407.2 206.5 %all-reduce.11.cloned.1.call-start = ((), (), s32[]{:S(2)}) async-start(), calls=%async_computation.9 | async-start | bytes 524288
  496.9 211.5 %reduce-scatter.10.cloned.1.call-start = ((), (), s32[]{:S(2)}) async-start(), calls=%async_computation.5 | async-start | bytes 278528 | tf_op jit(solution)/shard_map/reduce_scatter | solution.py:100
  614.4 4.7 collective-permute-start.4
  620.6 206.6 %all-reduce.13.cloned.1.call-start = ((), (), s32[]{:S(2)}) async-start(), calls=%async_computation.10 | async-start | bytes 524288
  710.4 208.9 %reduce-scatter.12.cloned.1.call-start = ((), (), s32[]{:S(2)}) async-start(), calls=%async_computation.6 | async-start | bytes 278528 | tf_op jit(solution)/shard_map/reduce_scatter | solution.py:100
  828.0 4.7 collective-permute-start.5
  834.2 203.9 %all-reduce.15.cloned.1.call-start = ((), (), s32[]{:S(2)}) async-start(), calls=%async_computation.11 | async-start | bytes 524288
  1058.4 2.6 copy-start.1
Sparse Core Ops, SparseCore 0:
  16.3 91.2 reduce-scatter.13
  258.4 141.0 all-reduce.8
  407.3 87.6 reduce-scatter.7
  498.8 114.7 all-reduce.10
  620.8 87.6 reduce-scatter.9
  712.3 114.8 all-reduce.12
  834.4 84.8 reduce-scatter.11
  923.4 114.7 all-reduce.14
where the time goes:
time: 1080 us; the launch traced here: 1070 us
  waiting for transfers between devices  830 us (77%)
  blocking collectives  154 us (14%)
  starting transfers between devices  34.2 us (3%)
  matrix products  22.1 us (2%)
  between operations  15.3 us (1%)
  local copies, waits for them, and re-layouts  13.9 us (1%)
    unnamed x13, waiting for transfers between devices  563 us
    reduce_scatter x3, waiting for transfers between devices, on_device(): lax.psum_scatter(partial_terms(jnp.int32(0), strip_rows * lax.axis_size('...  260 us
    all_gather x4, blocking collectives, on_device(): lax.all_gather(moved, 'rows', axis=0, tiled=True)  70.1 us
    all_gather x3, blocking collectives, on_device(): lax.all_gather(result, 'rows', axis=0, tiled=True)  49.3 us
    ppermute x6, starting transfers between devices, swapped(): return lax.ppermute(value, axis, pairs)  33.9 us
  transfers between devices with their start and end apart: 14, of which 14 were waited for; matrix products, arithmetic and copies ran while one was open for 0% of the time, Pallas kernels for 0%

commit v1 on v0

v1 whole, which is shorter than its diff:
```python
import functools

import jax
import jax.numpy as jnp
from jax import lax
from jax.experimental import pallas as pl
from jax.experimental.pallas import tpu as pltpu
from jax.sharding import PartitionSpec as P

MESH = pl.DeviceIdType.MESH
f32 = jnp.float32
bf16 = jnp.bfloat16

UNKNOWNS = 256
COLUMNS = 128
STRIP = 16
SHARE = 16
SHARES = 8
PEERS = 16
LOCALS = 3
LEVELS = 4
HALF = UNKNOWNS // 2
OCTET = 8
BLOCKS = (("inv", 0), ("low", 0, 0), ("low", 0, 1), ("inv", 1), ("low", 1, 0), ("low", 1, 1), ("inv", 2), ("low", 2, 0), ("inv", 3))
TRIOS = 3


def split(value):
    high = value.astype(bf16)
    return high, (value - high.astype(f32)).astype(bf16)


def dot(left, right, dim):
    return lax.dot_general(
        left, right, (((1,), (dim,)), ((), ())), preferred_element_type=f32
    )


def multiply(left, right, dim):
    return dot(left[0], right[0], dim) + dot(left[1], right[0], dim) + dot(left[0], right[1], dim)


def product(vectors, mat_high, mat_low, dim):
    return multiply(split(vectors), (mat_high, mat_low), dim)


def thin_product(vectors, mat_high, mat_low, dim):
    high = vectors.astype(bf16).astype(f32)
    both = jnp.concatenate([high, vectors - high], axis=0).astype(bf16)
    total = dot(both, mat_high, dim) + dot(both, mat_low, dim)
    return total[:SHARE] + total[SHARE:]


def regroup(tiles):
    group = lax.div(lax.broadcasted_iota(jnp.int32, (2, OCTET, 128), 2), STRIP)
    flat = tiles.reshape(PEERS * OCTET, 128)
    turned = [flat.reshape(2, 8, OCTET, 128)]
    for turn in range(1, 8):
        turned.append(pltpu.roll(flat, STRIP * turn, 1).reshape(2, 8, OCTET, 128))
    results = []
    for g in range(8):
        total = turned[-g % 8][:, 0]
        for m in range(1, 8):
            total = jnp.where(group == m, turned[(m - g) % 8][:, m], total)
        results.append(total)
    return results


def kinds_at(level):
    return 2 if level + 2 < LEVELS else 1


def inv_at(level):
    return BLOCKS.index(("inv", level))


def low_at(level, kind):
    return BLOCKS.index(("low", level, kind))


def trio(index):
    return slice(3 * index, 3 * index + 3)


def kernel(
    loc_names, loc_rhs, loc_inv, loc_low, lvl_rhs, lvl_inv, lvl_low, lvl_names,
    loc_out, sol_out,
    loc_parent, lvl_parent, rhs_s, inv_s, low_s, lvl_rhs_s, inv_high, inv_rest, low_high, low_rest, y_s,
    strips_s, snd, x_part, x_sum, y_part, y_sum, x_last, y_last, ride_snd, ride_rcv, names_snd, names_rcv,
    mats, mat_high, mat_rest, up_snd, up_rcv, down_snd, down_rcv,
    own_snd, ring_rcv, x_rcv, next_rcv, beside_rcv, sol_snd, sol_rcv, turned_s,
    load_sem, strips_sem, part_snd_sem, part_sem, last_snd_sem, last_sem,
    ride_snd_sem, ride_sem, names_snd_sem, names_sem, strip_snd_sem, strip_sem, ring_snd_sem, ring_sem, far_sem,
    pair_snd_sem, pair_sem, up_snd_sem, up_sem, down_snd_sem, down_sem, early_snd_sem, early_sem, late_snd_sem, late_sem,
    sol_snd_sem, sol_sem, beside_snd_sem, beside_sem,
):
    leaf = lax.axis_index("leaf")
    rows = lax.axis_index("rows")
    z, core = lax.div(leaf, 2), lax.rem(leaf, 2)
    y, x = lax.div(rows, 4), lax.rem(rows, 4)
    x_high, parity = lax.div(x, 2), lax.rem(x, 2)
    carried = 2 * z + x_high
    place = jnp.where(x_high == 0, parity, 1 - parity)
    share = 2 * y + core
    own = x_high == core

    def x_of(odd, slot):
        return 2 * odd + jnp.where(odd == 0, slot, 1 - slot)

    def around(value):
        return [value] + [jnp.where(value + n >= 4, value + n - 4, value + n) for n in range(1, 4)]

    slots, cores = [place, 1 - place], [core, 1 - core]
    ys, xs = around(y), around(x)
    carriers = [
        ((2 * z + there_core, 4 * there_y + x_of(core, slot)), 2 * there_y + there_core, slot)
        for there_y in ys
        for slot in slots
        for there_core in cores
    ]
    holders = [(carried, 4 * there_y + there_x) for there_y in ys for there_x in xs]
    x_carriers = [
        ((2 * z + there_core, 4 * y + x_of(core, slot)), slot, there_core)
        for slot in slots
        for there_core in cores
    ]
    x_holders = [(carried, 4 * y + there_x) for there_x in xs]
    sibling = (2 * z + 1 - core, rows)
    z_half = lax.rem(lax.div(z, 2), 2)
    beside = (leaf, rows + 1 - 2 * parity)
    partners = [[beside] + [(leaf, 4 * y + x_of(1 - x_high, slot)) for slot in range(2)]]
    for there_z in (z + 1 - 2 * lax.rem(z, 2), z + 2 - 4 * z_half):
        partners.append(
            [beside] + [(2 * there_z + core, 4 * y + x_of(x_high, slot)) for slot in range(2)]
        )
    y_up, y_far, y_down = ys[1], ys[2], ys[3]
    up, far, down = [(leaf, 4 * there_y + x) for there_y in (y_up, y_far, y_down)]

    loads = [
        pltpu.make_async_copy(loc_rhs, rhs_s, load_sem.at[0]),
        pltpu.make_async_copy(loc_inv, inv_s, load_sem.at[1]),
        pltpu.make_async_copy(loc_low, low_s, load_sem.at[2]),
        pltpu.make_async_copy(lvl_rhs, lvl_rhs_s, load_sem.at[3]),
        pltpu.make_async_copy(loc_names, loc_parent, load_sem.at[4]),
        pltpu.make_async_copy(lvl_names, lvl_parent, load_sem.at[5]),
    ]
    strip_loads = [
        pltpu.make_async_copy(
            lvl_inv.at[level], strips_s.at[:, inv_at(level)], strips_sem.at[inv_at(level)]
        )
        for level in range(LEVELS)
    ] + [
        pltpu.make_async_copy(
            lvl_low.at[level, :, 0 : kinds_at(level)],
            strips_s.at[:, low_at(level, 0) : low_at(level, 0) + kinds_at(level)],
            strips_sem.at[low_at(level, 0)],
        )
        for level in range(LEVELS - 1)
    ]
    for load in loads + strip_loads:
        load.start()

    barrier = pltpu.get_barrier_semaphore()

    def greet(device):
        pl.semaphore_signal(barrier, inc=1, device_id=device, device_id_type=MESH)

    others = [carrier[0] for carrier in carriers[1:]] + holders[1:] + [sibling, beside, up, far, down]
    others += [device for three in partners for device in three[1:]]
    for device in others:
        greet(device)

    @pl.when(jnp.logical_not(own))
    def _():
        greet(carriers[0][0])
        greet(holders[0])

    for load in loads[:2]:
        load.wait()
    for i in range(LOCALS):
        high, rest = split(inv_s[i])
        inv_high[i] = high
        inv_rest[i] = rest
        y_s[i] = product(rhs_s[i].T, high, rest, 1)
    pl.semaphore_wait(barrier, len(others) + jnp.where(own, 0, 2))

    def send(src, dst, send_sem, recv_sem, device):
        return pltpu.make_async_remote_copy(
            src_ref=src, dst_ref=dst, send_sem=send_sem, recv_sem=recv_sem,
            device_id=device, device_id_type=MESH,
        )

    def send_or_keep(copies):
        @pl.when(own)
        def _():
            for src, dst, send_sem, recv_sem, device in copies:
                pltpu.make_async_copy(src, dst, recv_sem).start()

        @pl.when(jnp.logical_not(own))
        def _():
            for copy in copies:
                send(*copy).start()

    def drain(ref, sem):
        pltpu.make_async_copy(ref, ref, sem).wait()

    strip = pl.ds(pl.multiple_of(STRIP * parity, STRIP), STRIP)
    first, second = slice(0, STRIP), slice(STRIP, 2 * STRIP)

    def along_x(index):
        copies = [
            (
                strips_s.at[slot, trio(index)], mats.at[trio(index), y, x_high, strip, :],
                strip_snd_sem, strip_sem.at[index], (2 * z + x_high, 4 * y + x_of(core, slot)),
            )
            for slot in slots
        ]
        send(*copies[1]).start()
        send_or_keep(copies[:1])

    def along_y(index):
        part = mats.at[trio(index), y, core]
        drain(part, strip_sem.at[index])
        for device in (up, down):
            send(part, part, ring_snd_sem, ring_sem.at[index], device).start()
        if index == 0:
            send(part, part, ring_snd_sem, far_sem.at[index], far).start()

    def to_far(index):
        drain(mats.at[trio(index), 0:2, core], ring_sem.at[index])
        for at_y, half_strip, device in ((y_down, first, up), (y_up, second, down)):
            part = mats.at[trio(index), at_y, core, half_strip, :]
            send(part, part, ring_snd_sem, far_sem.at[index], device).start()

    def to_sibling(index):
        if index == 0:
            drain(mats.at[trio(index), 0:2, core], ring_sem.at[index])
        drain(mats.at[trio(index), y_far, core], far_sem.at[index])
        part = mats.at[trio(index), :, core]
        send(part, part, pair_snd_sem, pair_sem.at[index], sibling).start()

    def take(index):
        drain(mats.at[trio(index), :, 1 - core], pair_sem.at[index])
        parts = {}
        for m in range(3 * index, 3 * index + 3):
            parts[BLOCKS[m]] = split(mats[m].reshape(UNKNOWNS, UNKNOWNS))
            if BLOCKS[m][0] == "inv":
                mat_high[m], mat_rest[m] = parts[BLOCKS[m]]
        for m in range(3 * index, 3 * index + 3):
            name, level = BLOCKS[m][:2]
            if name == "low":
                mat_high[m], mat_rest[m] = split(multiply(parts[BLOCKS[m]], parts["inv", level], 0))
            elif level + 1 == LEVELS:
                turned = split(mats[m].reshape(UNKNOWNS, UNKNOWNS).T)
                mat_high[m], mat_rest[m] = split(multiply(turned, parts[BLOCKS[m]], 0))

    def thin(vectors, m, dim):
        return thin_product(vectors, mat_high[m], mat_rest[m], dim)

    for load in strip_loads:
        load.wait()
    for index in range(TRIOS):
        along_x(index)
    for load in loads[2:]:
        load.wait()
    pick = [
        [jnp.where(loc_parent[i] == slot, 1.0, 0.0).astype(f32) for slot in range(2)]
        for i in range(LOCALS)
    ]

    y_others = [(up, y_up), (far, y_far), (down, y_down)]

    def local_updates(kind):
        for i in range(LOCALS):
            high, rest = split(low_s[i, kind])
            low_high[i, kind] = high
            low_rest[i, kind] = rest
            update = product(y_s[i], high, rest, 1).reshape(4, 2, SHARE, UNKNOWNS)
            for slot in range(2):
                if i == 0:
                    snd[kind, slot] = pick[i][slot] * update
                else:
                    snd[kind, slot] += pick[i][slot] * update

    def x_first():
        copies = [
            (snd.at[0, slot, :, there_core], x_part.at[x], part_snd_sem.at[0], part_sem.at[0], device)
            for device, slot, there_core in x_carriers
        ]
        for copy in copies[1:]:
            send(*copy).start()
        send_or_keep(copies[:1])

    def x_then_y():
        drain(x_part, part_sem.at[0])
        x_sum[...] = (x_part[0] + x_part[1]) + (x_part[2] + x_part[3])
        for device, there_y in y_others:
            send(
                x_sum.at[there_y], x_last.at[y], last_snd_sem.at[0], last_sem.at[0], device
            ).start()

    def y_first():
        for device, there_y in y_others:
            send(
                snd.at[1, :, there_y], y_part.at[y], part_snd_sem.at[1], part_sem.at[1], device
            ).start()

    def y_then_x():
        drain(y_part.at[0:3], part_sem.at[1])
        total = snd[1, :, y]
        for _, there_y in y_others:
            total = total + y_part[there_y]
        y_sum[...] = total
        copies = [
            (y_sum.at[slot, there_core], y_last.at[x], last_snd_sem.at[1], last_sem.at[1], device)
            for device, slot, there_core in x_carriers
        ]
        for copy in copies[1:]:
            send(*copy).start()
        send_or_keep(copies[:1])

    row = lax.broadcasted_iota(jnp.int32, (OCTET, 128), 0)
    names = jnp.zeros((OCTET, 128), f32)
    for k in range(2):
        for level in range(LEVELS - 1):
            names = jnp.where(row == 4 * k + level, lvl_parent[k, level].astype(f32), names)
    names_snd[...] = names
    send(names_snd, names_rcv, names_snd_sem, names_sem, sibling).start()
    for k in range(2):
        strips = [
            lvl_rhs_s[pl.ds(2 * STRIP * level + k, STRIP, stride=2), :] for level in range(LEVELS)
        ]
        strips.append(jnp.zeros((HALF - LEVELS * STRIP, COLUMNS), f32))
        extra = jnp.concatenate(strips, axis=0).T.reshape(SHARES, 2, OCTET, 128)
        right = pltpu.roll(extra[:, 1].reshape(SHARES * OCTET, 128), 64, 1)
        ride_snd[k] = extra[:, 0] + right.reshape(SHARES, OCTET, 128)
    rides = [
        (ride_snd.at[slot, index], ride_rcv.at[rows], ride_snd_sem, ride_sem, device)
        for device, index, slot in carriers
    ]
    for ride in rides[1:]:
        send(*ride).start()
    send_or_keep(rides[:1])
    local_updates(0)
    x_first()
    along_y(0)
    local_updates(1)
    y_first()
    along_y(1)
    along_y(2)
    x_then_y()

    def prepare_local(i):
        inverse = (inv_high[i], inv_rest[i])
        y_s[i] = product(y_s[i], inv_high[i], inv_rest[i], 0)
        for kind in range(2):
            high, rest = split(multiply((low_high[i, kind], low_rest[i, kind]), inverse, 0))
            low_high[i, kind] = high
            low_rest[i, kind] = rest

    to_sibling(0)
    to_far(1)

    y_then_x()
    drain(ride_rcv, ride_sem)
    parts = regroup(ride_rcv[...].reshape(2, 8, OCTET, 128))
    parts = [jnp.concatenate([part[0], part[1]], axis=1) for part in parts]
    rhs = [
        jnp.concatenate([parts[level], parts[LEVELS + level]], axis=0) for level in range(LEVELS)
    ]
    drain(names_rcv, names_sem)
    names = jnp.where(own, names_snd[...], names_rcv[...])
    parent = []
    for level in range(LEVELS - 1):
        name = jnp.where(place == 0, names[level : level + 1], names[4 + level : 5 + level])
        parent.append(jnp.broadcast_to(jnp.concatenate([name, name], axis=1), (SHARE, UNKNOWNS)))
    mine, places = place.astype(f32), [(1 - place).astype(f32), 2.0, 3.0]

    def chosen(name, at_place, value):
        return jnp.where(name == at_place, value, 0.0)

    def slot_at(index):
        return 0 if index == 0 else 1 + place

    def gathered(total, buffer, sem):
        drain(buffer, sem)
        for index in range(3):
            total = total + buffer[index]
        return total

    below = []
    take(0)
    to_sibling(1)
    drain(x_last.at[0:3], last_sem.at[0])
    above = x_sum[y]
    for _, there_y in y_others:
        above = above + x_last[there_y]
    for level in range(LEVELS):
        kinds = kinds_at(level)
        moved = rhs[level] - above
        if level + 1 < LEVELS:
            out = [thin(moved, low_at(level, kind), 1) for kind in range(kinds)]
            if level == 0:
                drain(y_last, last_sem.at[1])
                pending = (y_last[0] + y_last[1]) + (y_last[2] + y_last[3])
            else:
                pending = gathered(own_pending, up_rcv.at[level - 1, 1], up_sem.at[level - 1, 1])
            out[0] = out[0] + pending
            for kind in range(kinds):
                for index in range(3):
                    up_snd[level, kind, index] = chosen(parent[level], places[index], out[kind])
                    send(
                        up_snd.at[level, kind, index], up_rcv.at[level, kind, slot_at(index)],
                        up_snd_sem, up_sem.at[level, kind], partners[level][index],
                    ).start()
            own_pending = chosen(parent[level], mine, out[-1])
            if level == 0:
                to_far(2)
            below.append(thin(thin(moved, inv_at(level), 1), inv_at(level), 0))
            if level + 1 < TRIOS:
                take(level + 1)
            else:
                prepare_local(0)
            if level == 0:
                to_sibling(2)
            own_above = chosen(parent[level], mine, out[0])
            above = gathered(own_above, up_rcv.at[level, 0], up_sem.at[level, 0])

    def send_down(level, kind, value):
        down_snd[level, kind] = value
        for index in range(3):
            send(
                down_snd.at[level, kind], down_rcv.at[level, kind, slot_at(index)],
                down_snd_sem, down_sem.at[level, kind], partners[level][index],
            ).start()

    def pooled(level, kind, value):
        total = chosen(parent[level], mine, value)
        drain(down_rcv.at[level, kind], down_sem.at[level, kind])
        for index in range(3):
            total = total + chosen(parent[level], places[index], down_rcv[level, kind, index])
        return total

    def spread(step, landing, value):
        own_snd[step] = value.reshape(2, OCTET, UNKNOWNS)
        ring_rcv[step, y] = value[0:OCTET]
        for device, _ in y_others:
            send(
                own_snd.at[step, 0], ring_rcv.at[step, y],
                early_snd_sem.at[step], early_sem.at[step, 0], device,
            ).start()
        copies = [
            (
                own_snd.at[step, 1], landing.at[place, y, core, 1],
                early_snd_sem.at[step], early_sem.at[step, 1], device,
            )
            for device in x_holders
        ]
        for copy in copies[1:]:
            send(*copy).start()
        send_or_keep(copies[:1])

    def spread_on(step, landing):
        drain(ring_rcv.at[step, 0:3], early_sem.at[step, 0])
        copies = [
            (
                ring_rcv.at[step], landing.at[place, :, core, 0],
                late_snd_sem.at[step, 0], late_sem.at[step, 0], device,
            )
            for device in x_holders
        ]
        for copy in copies[1:]:
            send(*copy).start()
        send_or_keep(copies[:1])
        part = landing.at[:, y, :, 1]
        drain(part, early_sem.at[step, 1])
        for device, _ in y_others:
            send(part, part, late_snd_sem.at[step, 1], late_sem.at[step, 1], device).start()

    def spread_end(step, landing):
        drain(landing.at[:, :, :, 0], late_sem.at[step, 0])
        drain(landing.at[:, 0:3, :, 1], late_sem.at[step, 1])

    def whole(landing):
        return landing[...].reshape(2, COLUMNS, UNKNOWNS)

    current, current_parent = thin(moved, inv_at(LEVELS - 1), 0), None
    results = [None] * LEVELS
    results[LEVELS - 1] = current
    for level in range(LEVELS - 2, -1, -1):
        send_down(level, 0, current)
        if level == 0:
            spread(0, next_rcv, current)
            halves = []
            for octet in (slice(0, OCTET), slice(OCTET, SHARE)):
                for part in results[1:] + results[3:]:
                    halves.append(jnp.stack([part[octet, 0:HALF], part[octet, HALF:]], axis=0))
            tiles = regroup(jnp.stack(halves, axis=1))
            for m in range(8):
                for h in range(2):
                    sol_snd[8 * h + m] = tiles[m][h]
            spread_on(0, next_rcv)
            copies = [
                (sol_snd.at[device[1]], sol_rcv.at[place, share], sol_snd_sem, sol_sem, device)
                for device in holders
            ]
            for copy in copies[1:]:
                send(*copy).start()
            send_or_keep(copies[:1])
        else:
            prepare_local(LEVELS - 1 - level)
        left = below[level]
        if kinds_at(level) == 2:
            left = left - thin(pooled(level, 1, current_parent), low_at(level, 1), 0)
        current_parent = pooled(level, 0, current)
        if level > 0:
            send_down(level - 1, 1, current_parent)
        current = left - thin(current_parent, low_at(level, 0), 0)
        results[level] = current
    spread(1, x_rcv, current)

    spread_end(0, next_rcv)
    send(next_rcv, beside_rcv, beside_snd_sem, beside_sem, sibling).start()
    spread_on(1, x_rcv)
    drain(sol_rcv, sol_sem)
    for k in range(2):
        packed = sol_rcv[k].reshape(SHARES * OCTET, 128)
        right = pltpu.roll(packed, 64, 1).reshape(SHARES, OCTET, 128)
        both = jnp.stack([sol_rcv[k], right], axis=1).reshape(COLUMNS, 128)
        strips = both.T
        for level in range(1, LEVELS):
            to = pl.ds(2 * STRIP * level + k, STRIP, stride=2)
            sol_out[to, :] = strips[STRIP * (level - 1) : STRIP * level]
    drain(beside_rcv, beside_sem)
    own_next, beside_next = whole(next_rcv), whole(beside_rcv)
    for i in range(LOCALS):
        grand = None
        for at_place in range(4):
            weight = sum(
                pick[i][k] * jnp.where(lvl_parent[k, 0] == at_place, 1.0, 0.0).astype(f32)
                for k in range(2)
            )
            if at_place < 2:
                term = weight * own_next[at_place]
            else:
                term = weight * beside_next[at_place - 2]
            grand = term if grand is None else grand + term
        y_s[i] = y_s[i] - product(grand, low_high[i, 1], low_rest[i, 1], 0)
    spread_end(1, x_rcv)
    x_all = whole(x_rcv)
    for i in range(LOCALS):
        above_x = pick[i][0] * x_all[0] + pick[i][1] * x_all[1]
        loc_out[i] = (y_s[i] - product(above_x, low_high[i, 0], low_rest[i, 0], 0)).T
    here = pl.ds(pl.multiple_of(STRIP * rows, STRIP), STRIP)
    for k in range(2):
        turned_s[k] = x_all[k].T
        sol_out[pl.ds(k, STRIP, stride=2), :] = turned_s[k, here, :]

    drain(x_part.at[0:3], part_snd_sem.at[0])
    drain(y_part.at[0:3], part_snd_sem.at[1])
    drain(x_last.at[0:3], last_snd_sem.at[0])
    drain(y_last.at[0:3], last_snd_sem.at[1])
    drain(ride_rcv.at[1:], ride_snd_sem)
    drain(names_snd, names_snd_sem)
    for step in range(2):
        for _ in range(2):
            drain(ring_rcv.at[step, 0:3], early_snd_sem.at[step])
        for _ in range(3):
            drain(ring_rcv.at[step], late_snd_sem.at[step, 0])
        drain(x_rcv.at[:, 0:3, :, 1], late_snd_sem.at[step, 1])
    drain(sol_snd.at[1:], sol_snd_sem)
    drain(strips_s.at[0], strip_snd_sem)
    drain(mats.at[:, 0:3, 0], ring_snd_sem)
    drain(mats.at[:, :, 0], pair_snd_sem)
    drain(beside_rcv, beside_snd_sem)
    for level in range(LEVELS - 1):
        for kind in range(kinds_at(level)):
            drain(up_rcv.at[level, kind], up_snd_sem)
            drain(down_rcv.at[level, kind], down_snd_sem)

    @pl.when(jnp.logical_not(own))
    def _():
        drain(x_part.at[0], part_snd_sem.at[0])
        drain(y_last.at[0], last_snd_sem.at[1])
        drain(ride_rcv.at[0], ride_snd_sem)
        for step in range(2):
            drain(ring_rcv.at[step, 0], early_snd_sem.at[step])
            drain(ring_rcv.at[step], late_snd_sem.at[step, 0])
        drain(sol_snd.at[0], sol_snd_sem)
        drain(strips_s.at[0], strip_snd_sem)


def on_device(loc_rhs, loc_inv, loc_low, loc_parent, lvl_rhs, lvl_inv, lvl_low, lvl_parent):
    vmem = pl.BlockSpec(memory_space=pltpu.VMEM)
    far = pl.BlockSpec(memory_space=pltpu.HBM)
    dma = pltpu.SemaphoreType.DMA
    square = (UNKNOWNS, UNKNOWNS)
    loc_sol, sol = pl.pallas_call(
        kernel,
        out_shape=(
            jax.ShapeDtypeStruct((LOCALS, UNKNOWNS, COLUMNS), f32),
            jax.ShapeDtypeStruct((COLUMNS, 128), f32),
        ),
        in_specs=[far] * 8,
        out_specs=(vmem, vmem),
        scratch_shapes=[
            pltpu.SMEM((LOCALS,), jnp.int32),
            pltpu.SMEM((2, LEVELS - 1), jnp.int32),
            pltpu.VMEM((LOCALS, UNKNOWNS, COLUMNS), f32),
            pltpu.VMEM((LOCALS,) + square, f32),
            pltpu.VMEM((LOCALS, 2) + square, f32),
            pltpu.VMEM((LEVELS * STRIP * 2, COLUMNS), f32),
            pltpu.VMEM((LOCALS,) + square, bf16),
            pltpu.VMEM((LOCALS,) + square, bf16),
            pltpu.VMEM((LOCALS, 2) + square, bf16),
            pltpu.VMEM((LOCALS, 2) + square, bf16),
            pltpu.VMEM((LOCALS, COLUMNS, UNKNOWNS), f32),
            pltpu.VMEM((2, len(BLOCKS), STRIP, UNKNOWNS), f32),
            pltpu.VMEM((2, 2, 4, 2, SHARE, UNKNOWNS), f32),
            pltpu.VMEM((4, 4, SHARE, UNKNOWNS), f32),
            pltpu.VMEM((4, SHARE, UNKNOWNS), f32),
            pltpu.VMEM((4, 2, 2, SHARE, UNKNOWNS), f32),
            pltpu.VMEM((2, 2, SHARE, UNKNOWNS), f32),
            pltpu.VMEM((4, SHARE, UNKNOWNS), f32),
            pltpu.VMEM((4, SHARE, UNKNOWNS), f32),
            pltpu.VMEM((2, SHARES, OCTET, 128), f32),
            pltpu.VMEM((PEERS, OCTET, 128), f32),
            pltpu.VMEM((OCTET, 128), f32),
            pltpu.VMEM((OCTET, 128), f32),
            pltpu.VMEM((len(BLOCKS), 4, 2, 2 * STRIP, UNKNOWNS), f32),
            pltpu.VMEM((len(BLOCKS),) + square, bf16),
            pltpu.VMEM((len(BLOCKS),) + square, bf16),
            pltpu.VMEM((LEVELS - 1, 2, 3, SHARE, UNKNOWNS), f32),
            pltpu.VMEM((LEVELS - 1, 2, 3, SHARE, UNKNOWNS), f32),
            pltpu.VMEM((LEVELS - 1, 2, SHARE, UNKNOWNS), f32),
            pltpu.VMEM((LEVELS - 1, 2, 3, SHARE, UNKNOWNS), f32),
            pltpu.VMEM((2, 2, OCTET, UNKNOWNS), f32),
            pltpu.VMEM((2, 4, OCTET, UNKNOWNS), f32),
            pltpu.VMEM((2, 4, 2, 2, OCTET, UNKNOWNS), f32),
            pltpu.VMEM((2, 4, 2, 2, OCTET, UNKNOWNS), f32),
            pltpu.VMEM((2, 4, 2, 2, OCTET, UNKNOWNS), f32),
            pltpu.VMEM((PEERS, OCTET, 128), f32),
            pltpu.VMEM((2, SHARES, OCTET, 128), f32),
            pltpu.VMEM((2, UNKNOWNS, COLUMNS), f32),
            dma((6,)),
            dma((len(BLOCKS),)),
            dma((2,)),
            dma((2,)),
            dma((2,)),
            dma((2,)),
            dma,
            dma,
            dma,
            dma,
            dma,
            dma((TRIOS,)),
            dma,
            dma((TRIOS,)),
            dma((TRIOS,)),
            dma,
            dma((TRIOS,)),
            dma,
            dma((LEVELS - 1, 2)),
            dma,
            dma((LEVELS - 1, 2)),
            dma((2,)),
            dma((2, 2)),
            dma((2, 2)),
            dma((2, 2)),
            dma,
            dma,
            dma,
            dma,
        ],
        compiler_params=pltpu.CompilerParams(
            collective_id=0, has_side_effects=True, vmem_limit_bytes=40 * 1024 * 1024
        ),
    )(
        *(
            pltpu.with_memory_space_constraint(operand, pltpu.HBM)
            for operand in (
                loc_parent.reshape(LOCALS),
                loc_rhs.reshape(LOCALS, UNKNOWNS, COLUMNS),
                loc_inv.reshape((LOCALS,) + square),
                loc_low.reshape((LOCALS, 2) + square),
                lvl_rhs.reshape(LEVELS * STRIP * 2, COLUMNS),
                lvl_inv.reshape(LEVELS, 2, STRIP, UNKNOWNS),
                lvl_low.reshape(LEVELS - 1, 2, 2, STRIP, UNKNOWNS),
                lvl_parent.reshape(LEVELS - 1, 2).T,
            )
        )
    )
    return loc_sol[None, None], sol.reshape(1, LEVELS, STRIP, 2, COLUMNS)


def solution(mesh):
    in_specs = (
        P("leaf", "rows", None, None, None),
        P("leaf", "rows", None, None, None),
        P("leaf", "rows", None, None, None, None),
        P("leaf", "rows", None),
        P("leaf", None, "rows", None, None),
        P("leaf", None, None, "rows", None),
        P("leaf", None, None, None, "rows", None),
        P("leaf", None, None),
    )
    out_specs = (P("leaf", "rows", None, None, None), P("leaf", None, "rows", None, None))
    return jax.shard_map(
        on_device, mesh=mesh, in_specs=in_specs, out_specs=out_specs, check_vma=False
    )
```

time: 1080 us -> 65.6 us (0.06)
  waiting for transfers between devices: 830 us -> 0 us
  blocking collectives: 154 us -> 0 us
  Pallas kernels: 0 us -> 63.4 us
  starting transfers between devices: 34.2 us -> 0 us
  matrix products: 22.1 us -> 0 us
  between operations: 15.3 us -> 0.64 us
  local copies, waits for them, and re-layouts: 13.9 us -> 1.38 us
    unnamed x13 -> x0, waiting for transfers between devices: 563 us -> none
    reduce_scatter x3 -> x0, waiting for transfers between devices: 260 us -> none  [on_device(): lax.psum_scatter(partial_terms(jnp.int32(0), strip_rows * lax.axis_size('...]
    all_gather x9 -> x0, blocking collectives: 154 us -> none  [the longest x4 70.1 us: on_device(): lax.all_gather(moved, 'rows', axis=0, tiled=True)]
    pallas_call x0 -> x1, Pallas kernels: none -> 63.4 us  [on_device(): pl.pallas_call(kernel, out_shape=(jax.ShapeDtypeStruct((LOCALS, UNKNOWNS,...]
    ppermute x6 -> x0, starting transfers between devices: 33.9 us -> none  [swapped(): return lax.ppermute(value, axis, pairs)]
    dot_general x27 -> x0, matrix products: 22.1 us -> none  [the longest x3 3.89 us: partial_terms(): return jnp.einsum('kjbc,bkjn->ckn', low_used, above_x, precision=precise)]
  transfers between devices with their start and end apart: 14 -> 0, of which waited for: 14 -> 0; matrix products, arithmetic and copies ran while one was open for 0% -> 0% of each run, Pallas kernels for 0% -> 0%
where the time goes in v1:
time: 65.6 us; the launch traced here: 65.4 us
  Pallas kernels  63.4 us (97%)
  local copies, waits for them, and re-layouts  1.38 us (2%)
    pallas_call x1, Pallas kernels, on_device(): pl.pallas_call(kernel, out_shape=(jax.ShapeDtypeStruct((LOCALS, UNKNOWNS,...  63.4 us
    unnamed x2, local copies, waits for them, and re-layouts  1.38 us

profile of v1, /device:TPU:1, one launch (start us, length us, event | category | flops | bytes accessed | tf_op | source)
XLA Modules:
  0.0 65.4 jit_solution(437502975560502144)
XLA Ops:
  0.6 63.4 %shard_map.95 = (f32[3,256,128]{2,1,0:T(8,128)S(1)}, f32[128,128]{1,0:T(8,128)S(1)}) custom-call(s32[3]{0:T(128)} %bitcast.21, f32[3,256,128]{2,1,0:T(8,128)} %bitcast.16, f32[3,256,256]{2,1,0:T(8,128)} %bitcast.15, f32[3,2,256,256]{3,2,1,0:T(8,128)} %bitcast.14, f32[128,128]{1,0:T(8,128)} %bitcast.19, f32[4,2,16,256]{3,2,1,0:T(8,128)} %bitcast.18, ...), custom_call_target="tpu_custom_call" | custom-call | tf_op jit(solution)/shard_map/pallas_call | solution.py:598
  64.0 0.7 %copy.12 = f32[1,1,3,256,128]{4,3,2,1,0:T(8,128)} copy(f32[1,1,3,256,128]{4,3,2,1,0:T(8,128)S(1)} %bitcast.12) | data formatting | bytes 786432
  64.8 0.6 copy.13

commit v2 on v1

--- a/solution.py
+++ b/solution.py
@@ -91,7 +91,7 @@
     own_snd, ring_rcv, x_rcv, next_rcv, beside_rcv, sol_snd, sol_rcv, turned_s,
     load_sem, strips_sem, part_snd_sem, part_sem, last_snd_sem, last_sem,
     ride_snd_sem, ride_sem, names_snd_sem, names_sem, strip_snd_sem, strip_sem, ring_snd_sem, ring_sem, far_sem,
-    pair_snd_sem, pair_sem, up_snd_sem, up_sem, down_snd_sem, down_sem, early_snd_sem, early_sem, late_snd_sem, late_sem,
+    up_snd_sem, up_sem, down_snd_sem, down_sem, early_snd_sem, early_sem, late_snd_sem, late_sem,
     sol_snd_sem, sol_sem, beside_snd_sem, beside_sem,
 ):
     leaf = lax.axis_index("leaf")
@@ -99,40 +99,34 @@
     z, core = lax.div(leaf, 2), lax.rem(leaf, 2)
     y, x = lax.div(rows, 4), lax.rem(rows, 4)
     x_high, parity = lax.div(x, 2), lax.rem(x, 2)
-    carried = 2 * z + x_high
-    place = jnp.where(x_high == 0, parity, 1 - parity)
-    share = 2 * y + core
-    own = x_high == core
-
-    def x_of(odd, slot):
-        return 2 * odd + jnp.where(odd == 0, slot, 1 - slot)
+    carried = 2 * z + parity
+    share = 2 * y + x_high
+    own = parity == core
 
     def around(value):
         return [value] + [jnp.where(value + n >= 4, value + n - 4, value + n) for n in range(1, 4)]
 
-    slots, cores = [place, 1 - place], [core, 1 - core]
+    slots, halves = [core, 1 - core], [x_high, 1 - x_high]
     ys, xs = around(y), around(x)
     carriers = [
-        ((2 * z + there_core, 4 * there_y + x_of(core, slot)), 2 * there_y + there_core, slot)
+        ((2 * z + slot, 4 * there_y + 2 * half + core), 2 * there_y + half, slot)
         for there_y in ys
+        for half in halves
         for slot in slots
-        for there_core in cores
     ]
     holders = [(carried, 4 * there_y + there_x) for there_y in ys for there_x in xs]
     x_carriers = [
-        ((2 * z + there_core, 4 * y + x_of(core, slot)), slot, there_core)
-        for slot in slots
-        for there_core in cores
+        ((2 * z + slot, 4 * y + 2 * half + core), slot, half) for half in halves for slot in slots
     ]
     x_holders = [(carried, 4 * y + there_x) for there_x in xs]
     sibling = (2 * z + 1 - core, rows)
     z_half = lax.rem(lax.div(z, 2), 2)
-    beside = (leaf, rows + 1 - 2 * parity)
-    partners = [[beside] + [(leaf, 4 * y + x_of(1 - x_high, slot)) for slot in range(2)]]
-    for there_z in (z + 1 - 2 * lax.rem(z, 2), z + 2 - 4 * z_half):
-        partners.append(
-            [beside] + [(2 * there_z + core, 4 * y + x_of(x_high, slot)) for slot in range(2)]
+    partners = [
+        [sibling] + [(2 * there_z + slot, there_rows) for slot in range(2)]
+        for there_z, there_rows in (
+            (z, rows + 1 - 2 * parity), (z + 1 - 2 * lax.rem(z, 2), rows), (z + 2 - 4 * z_half, rows)
         )
+    ]
     y_up, y_far, y_down = ys[1], ys[2], ys[3]
     up, far, down = [(leaf, 4 * there_y + x) for there_y in (y_up, y_far, y_down)]
 
@@ -165,7 +159,7 @@
     def greet(device):
         pl.semaphore_signal(barrier, inc=1, device_id=device, device_id_type=MESH)
 
-    others = [carrier[0] for carrier in carriers[1:]] + holders[1:] + [sibling, beside, up, far, down]
+    others = [carrier[0] for carrier in carriers[1:]] + holders[1:] + [sibling, up, far, down]
     others += [device for three in partners for device in three[1:]]
     for device in others:
         greet(device)
@@ -204,43 +198,35 @@
     def drain(ref, sem):
         pltpu.make_async_copy(ref, ref, sem).wait()
 
-    strip = pl.ds(pl.multiple_of(STRIP * parity, STRIP), STRIP)
-    first, second = slice(0, STRIP), slice(STRIP, 2 * STRIP)
+    strip = pl.ds(pl.multiple_of(STRIP * x, STRIP), STRIP)
+    first, second = slice(0, 2 * STRIP), slice(2 * STRIP, 4 * STRIP)
 
     def along_x(index):
         copies = [
             (
-                strips_s.at[slot, trio(index)], mats.at[trio(index), y, x_high, strip, :],
-                strip_snd_sem, strip_sem.at[index], (2 * z + x_high, 4 * y + x_of(core, slot)),
+                strips_s.at[slot, trio(index)], mats.at[trio(index), y, strip, :],
+                strip_snd_sem, strip_sem.at[index], device,
             )
-            for slot in slots
+            for device, slot, _ in x_carriers
         ]
-        send(*copies[1]).start()
+        for copy in copies[1:]:
+            send(*copy).start()
         send_or_keep(copies[:1])
 
     def along_y(index):
-        part = mats.at[trio(index), y, core]
+        part = mats.at[trio(index), y]
         drain(part, strip_sem.at[index])
         for device in (up, down):
             send(part, part, ring_snd_sem, ring_sem.at[index], device).start()
-        if index == 0:
-            send(part, part, ring_snd_sem, far_sem.at[index], far).start()
 
     def to_far(index):
-        drain(mats.at[trio(index), 0:2, core], ring_sem.at[index])
+        drain(mats.at[trio(index), 0:2], ring_sem.at[index])
         for at_y, half_strip, device in ((y_down, first, up), (y_up, second, down)):
-            part = mats.at[trio(index), at_y, core, half_strip, :]
+            part = mats.at[trio(index), at_y, half_strip, :]
             send(part, part, ring_snd_sem, far_sem.at[index], device).start()
 
-    def to_sibling(index):
-        if index == 0:
-            drain(mats.at[trio(index), 0:2, core], ring_sem.at[index])
-        drain(mats.at[trio(index), y_far, core], far_sem.at[index])
-        part = mats.at[trio(index), :, core]
-        send(part, part, pair_snd_sem, pair_sem.at[index], sibling).start()
-
     def take(index):
-        drain(mats.at[trio(index), :, 1 - core], pair_sem.at[index])
+        drain(mats.at[trio(index), y_far], far_sem.at[index])
         parts = {}
         for m in range(3 * index, 3 * index + 3):
             parts[BLOCKS[m]] = split(mats[m].reshape(UNKNOWNS, UNKNOWNS))
@@ -284,8 +270,8 @@
 
     def x_first():
         copies = [
-            (snd.at[0, slot, :, there_core], x_part.at[x], part_snd_sem.at[0], part_sem.at[0], device)
-            for device, slot, there_core in x_carriers
+            (snd.at[0, slot, :, half], x_part.at[x], part_snd_sem.at[0], part_sem.at[0], device)
+            for device, slot, half in x_carriers
         ]
         for copy in copies[1:]:
             send(*copy).start()
@@ -312,8 +298,8 @@
             total = total + y_part[there_y]
         y_sum[...] = total
         copies = [
-            (y_sum.at[slot, there_core], y_last.at[x], last_snd_sem.at[1], last_sem.at[1], device)
-            for device, slot, there_core in x_carriers
+            (y_sum.at[slot, half], y_last.at[x], last_snd_sem.at[1], last_sem.at[1], device)
+            for device, slot, half in x_carriers
         ]
         for copy in copies[1:]:
             send(*copy).start()
@@ -347,8 +333,9 @@
     local_updates(1)
     y_first()
     along_y(1)
+    x_then_y()
+    to_far(0)
     along_y(2)
-    x_then_y()
 
     def prepare_local(i):
         inverse = (inv_high[i], inv_rest[i])
@@ -358,9 +345,6 @@
             low_high[i, kind] = high
             low_rest[i, kind] = rest
 
-    to_sibling(0)
-    to_far(1)
-
     y_then_x()
     drain(ride_rcv, ride_sem)
     parts = regroup(ride_rcv[...].reshape(2, 8, OCTET, 128))
@@ -372,15 +356,15 @@
     names = jnp.where(own, names_snd[...], names_rcv[...])
     parent = []
     for level in range(LEVELS - 1):
-        name = jnp.where(place == 0, names[level : level + 1], names[4 + level : 5 + level])
+        name = jnp.where(core == 0, names[level : level + 1], names[4 + level : 5 + level])
         parent.append(jnp.broadcast_to(jnp.concatenate([name, name], axis=1), (SHARE, UNKNOWNS)))
-    mine, places = place.astype(f32), [(1 - place).astype(f32), 2.0, 3.0]
+    mine, places = core.astype(f32), [(1 - core).astype(f32), 2.0, 3.0]
 
     def chosen(name, at_place, value):
         return jnp.where(name == at_place, value, 0.0)
 
     def slot_at(index):
-        return 0 if index == 0 else 1 + place
+        return 0 if index == 0 else 1 + core
 
     def gathered(total, buffer, sem):
         drain(buffer, sem)
@@ -390,7 +374,7 @@
 
     below = []
     take(0)
-    to_sibling(1)
+    to_far(1)
     drain(x_last.at[0:3], last_sem.at[0])
     above = x_sum[y]
     for _, there_y in y_others:
@@ -421,8 +405,6 @@
                 take(level + 1)
             else:
                 prepare_local(0)
-            if level == 0:
-                to_sibling(2)
             own_above = chosen(parent[level], mine, out[0])
             above = gathered(own_above, up_rcv.at[level, 0], up_sem.at[level, 0])
 
@@ -451,7 +433,7 @@
             ).start()
         copies = [
             (
-                own_snd.at[step, 1], landing.at[place, y, core, 1],
+                own_snd.at[step, 1], landing.at[core, y, x_high, 1],
                 early_snd_sem.at[step], early_sem.at[step, 1], device,
             )
             for device in x_holders
@@ -464,7 +446,7 @@
         drain(ring_rcv.at[step, 0:3], early_sem.at[step, 0])
         copies = [
             (
-                ring_rcv.at[step], landing.at[place, :, core, 0],
+                ring_rcv.at[step], landing.at[core, :, x_high, 0],
                 late_snd_sem.at[step, 0], late_sem.at[step, 0], device,
             )
             for device in x_holders
@@ -501,7 +483,7 @@
                     sol_snd[8 * h + m] = tiles[m][h]
             spread_on(0, next_rcv)
             copies = [
-                (sol_snd.at[device[1]], sol_rcv.at[place, share], sol_snd_sem, sol_sem, device)
+                (sol_snd.at[device[1]], sol_rcv.at[core, share], sol_snd_sem, sol_sem, device)
                 for device in holders
             ]
             for copy in copies[1:]:
@@ -569,9 +551,9 @@
             drain(ring_rcv.at[step], late_snd_sem.at[step, 0])
         drain(x_rcv.at[:, 0:3, :, 1], late_snd_sem.at[step, 1])
     drain(sol_snd.at[1:], sol_snd_sem)
-    drain(strips_s.at[0], strip_snd_sem)
-    drain(mats.at[:, 0:3, 0], ring_snd_sem)
-    drain(mats.at[:, :, 0], pair_snd_sem)
+    for _ in range(3):
+        drain(strips_s.at[0], strip_snd_sem)
+    drain(mats.at[:, 0:3], ring_snd_sem)
     drain(beside_rcv, beside_snd_sem)
     for level in range(LEVELS - 1):
         for kind in range(kinds_at(level)):
@@ -627,7 +609,7 @@
             pltpu.VMEM((PEERS, OCTET, 128), f32),
             pltpu.VMEM((OCTET, 128), f32),
             pltpu.VMEM((OCTET, 128), f32),
-            pltpu.VMEM((len(BLOCKS), 4, 2, 2 * STRIP, UNKNOWNS), f32),
+            pltpu.VMEM((len(BLOCKS), 4, 4 * STRIP, UNKNOWNS), f32),
             pltpu.VMEM((len(BLOCKS),) + square, bf16),
             pltpu.VMEM((len(BLOCKS),) + square, bf16),
             pltpu.VMEM((LEVELS - 1, 2, 3, SHARE, UNKNOWNS), f32),
@@ -658,8 +640,6 @@
             dma((TRIOS,)),
             dma((TRIOS,)),
             dma,
-            dma((TRIOS,)),
-            dma,
             dma((LEVELS - 1, 2)),
             dma,
             dma((LEVELS - 1, 2)),

time: 65.6 us -> 68.1 us (1.038)
  Pallas kernels: 63.4 us -> 65.9 us
    pallas_call x1, Pallas kernels: 63.4 us -> 65.9 us  [on_device(): pl.pallas_call(kernel, out_shape=(jax.ShapeDtypeStruct((LOCALS, UNKNOWNS,...]
where the time goes in v2:
time: 68.1 us; the launch traced here: 67.9 us
  Pallas kernels  65.9 us (97%)
  local copies, waits for them, and re-layouts  1.38 us (2%)
    pallas_call x1, Pallas kernels, on_device(): pl.pallas_call(kernel, out_shape=(jax.ShapeDtypeStruct((LOCALS, UNKNOWNS,...  65.9 us
    unnamed x2, local copies, waits for them, and re-layouts  1.38 us

profile of v2, /device:TPU:1, one launch (start us, length us, event | category | flops | bytes accessed | tf_op | source)
XLA Modules:
  0.0 67.9 jit_solution(13219143779279585894)
XLA Ops:
  0.6 65.9 %shard_map.95 = (f32[3,256,128]{2,1,0:T(8,128)S(1)}, f32[128,128]{1,0:T(8,128)S(1)}) custom-call(s32[3]{0:T(128)} %bitcast.21, f32[3,256,128]{2,1,0:T(8,128)} %bitcast.16, f32[3,256,256]{2,1,0:T(8,128)} %bitcast.15, f32[3,2,256,256]{3,2,1,0:T(8,128)} %bitcast.14, f32[128,128]{1,0:T(8,128)} %bitcast.19, f32[4,2,16,256]{3,2,1,0:T(8,128)} %bitcast.18, ...), custom_call_target="tpu_custom_call" | custom-call | tf_op jit(solution)/shard_map/pallas_call | solution.py:580
  66.5 0.7 %copy.12 = f32[1,1,3,256,128]{4,3,2,1,0:T(8,128)} copy(f32[1,1,3,256,128]{4,3,2,1,0:T(8,128)S(1)} %bitcast.12) | data formatting | bytes 786432
  67.3 0.6 copy.13

commit v3 on v1

--- a/solution.py
+++ b/solution.py
@@ -259,8 +259,7 @@
 
     for load in strip_loads:
         load.wait()
-    for index in range(TRIOS):
-        along_x(index)
+    along_x(0)
     for load in loads[2:]:
         load.wait()
     pick = [
@@ -319,6 +318,13 @@
             send(*copy).start()
         send_or_keep(copies[:1])
 
+    local_updates(0)
+    x_first()
+    along_y(0)
+    along_x(1)
+    along_x(2)
+    local_updates(1)
+    y_first()
     row = lax.broadcasted_iota(jnp.int32, (OCTET, 128), 0)
     names = jnp.zeros((OCTET, 128), f32)
     for k in range(2):
@@ -341,14 +347,9 @@
     for ride in rides[1:]:
         send(*ride).start()
     send_or_keep(rides[:1])
-    local_updates(0)
-    x_first()
-    along_y(0)
-    local_updates(1)
-    y_first()
     along_y(1)
+    x_then_y()
     along_y(2)
-    x_then_y()
 
     def prepare_local(i):
         inverse = (inv_high[i], inv_rest[i])
@@ -359,8 +360,6 @@
             low_rest[i, kind] = rest
 
     to_sibling(0)
-    to_far(1)
-
     y_then_x()
     drain(ride_rcv, ride_sem)
     parts = regroup(ride_rcv[...].reshape(2, 8, OCTET, 128))
@@ -390,7 +389,7 @@
 
     below = []
     take(0)
-    to_sibling(1)
+    to_far(1)
     drain(x_last.at[0:3], last_sem.at[0])
     above = x_sum[y]
     for _, there_y in y_others:
@@ -415,6 +414,7 @@
                     ).start()
             own_pending = chosen(parent[level], mine, out[-1])
             if level == 0:
+                to_sibling(1)
                 to_far(2)
             below.append(thin(thin(moved, inv_at(level), 1), inv_at(level), 0))
             if level + 1 < TRIOS:
@@ -491,22 +491,7 @@
         send_down(level, 0, current)
         if level == 0:
             spread(0, next_rcv, current)
-            halves = []
-            for octet in (slice(0, OCTET), slice(OCTET, SHARE)):
-                for part in results[1:] + results[3:]:
-                    halves.append(jnp.stack([part[octet, 0:HALF], part[octet, HALF:]], axis=0))
-            tiles = regroup(jnp.stack(halves, axis=1))
-            for m in range(8):
-                for h in range(2):
-                    sol_snd[8 * h + m] = tiles[m][h]
             spread_on(0, next_rcv)
-            copies = [
-                (sol_snd.at[device[1]], sol_rcv.at[place, share], sol_snd_sem, sol_sem, device)
-                for device in holders
-            ]
-            for copy in copies[1:]:
-                send(*copy).start()
-            send_or_keep(copies[:1])
         else:
             prepare_local(LEVELS - 1 - level)
         left = below[level]
@@ -521,16 +506,22 @@
 
     spread_end(0, next_rcv)
     send(next_rcv, beside_rcv, beside_snd_sem, beside_sem, sibling).start()
+    halves = []
+    for octet in (slice(0, OCTET), slice(OCTET, SHARE)):
+        for part in results[1:] + results[3:]:
+            halves.append(jnp.stack([part[octet, 0:HALF], part[octet, HALF:]], axis=0))
+    tiles = regroup(jnp.stack(halves, axis=1))
+    for m in range(8):
+        for h in range(2):
+            sol_snd[8 * h + m] = tiles[m][h]
     spread_on(1, x_rcv)
-    drain(sol_rcv, sol_sem)
-    for k in range(2):
-        packed = sol_rcv[k].reshape(SHARES * OCTET, 128)
-        right = pltpu.roll(packed, 64, 1).reshape(SHARES, OCTET, 128)
-        both = jnp.stack([sol_rcv[k], right], axis=1).reshape(COLUMNS, 128)
-        strips = both.T
-        for level in range(1, LEVELS):
-            to = pl.ds(2 * STRIP * level + k, STRIP, stride=2)
-            sol_out[to, :] = strips[STRIP * (level - 1) : STRIP * level]
+    copies = [
+        (sol_snd.at[device[1]], sol_rcv.at[place, share], sol_snd_sem, sol_sem, device)
+        for device in holders
+    ]
+    for copy in copies[1:]:
+        send(*copy).start()
+    send_or_keep(copies[:1])
     drain(beside_rcv, beside_sem)
     own_next, beside_next = whole(next_rcv), whole(beside_rcv)
     for i in range(LOCALS):
@@ -546,16 +537,6 @@
                 term = weight * beside_next[at_place - 2]
             grand = term if grand is None else grand + term
         y_s[i] = y_s[i] - product(grand, low_high[i, 1], low_rest[i, 1], 0)
-    spread_end(1, x_rcv)
-    x_all = whole(x_rcv)
-    for i in range(LOCALS):
-        above_x = pick[i][0] * x_all[0] + pick[i][1] * x_all[1]
-        loc_out[i] = (y_s[i] - product(above_x, low_high[i, 0], low_rest[i, 0], 0)).T
-    here = pl.ds(pl.multiple_of(STRIP * rows, STRIP), STRIP)
-    for k in range(2):
-        turned_s[k] = x_all[k].T
-        sol_out[pl.ds(k, STRIP, stride=2), :] = turned_s[k, here, :]
-
     drain(x_part.at[0:3], part_snd_sem.at[0])
     drain(y_part.at[0:3], part_snd_sem.at[1])
     drain(x_last.at[0:3], last_snd_sem.at[0])
@@ -588,6 +569,25 @@
             drain(ring_rcv.at[step], late_snd_sem.at[step, 0])
         drain(sol_snd.at[0], sol_snd_sem)
         drain(strips_s.at[0], strip_snd_sem)
+
+    spread_end(1, x_rcv)
+    x_all = whole(x_rcv)
+    for i in range(LOCALS):
+        above_x = pick[i][0] * x_all[0] + pick[i][1] * x_all[1]
+        loc_out[i] = (y_s[i] - product(above_x, low_high[i, 0], low_rest[i, 0], 0)).T
+    here = pl.ds(pl.multiple_of(STRIP * rows, STRIP), STRIP)
+    for k in range(2):
+        turned_s[k] = x_all[k].T
+        sol_out[pl.ds(k, STRIP, stride=2), :] = turned_s[k, here, :]
+    drain(sol_rcv, sol_sem)
+    for k in range(2):
+        packed = sol_rcv[k].reshape(SHARES * OCTET, 128)
+        right = pltpu.roll(packed, 64, 1).reshape(SHARES, OCTET, 128)
+        both = jnp.stack([sol_rcv[k], right], axis=1).reshape(COLUMNS, 128)
+        strips = both.T
+        for level in range(1, LEVELS):
+            to = pl.ds(2 * STRIP * level + k, STRIP, stride=2)
+            sol_out[to, :] = strips[STRIP * (level - 1) : STRIP * level]
 
 
 def on_device(loc_rhs, loc_inv, loc_low, loc_parent, lvl_rhs, lvl_inv, lvl_low, lvl_parent):

time: 65.6 us -> 65.5 us (level)
  no operation moved by 1% of the time
where the time goes in v3:
time: 65.5 us; the launch traced here: 65.4 us
  Pallas kernels  63.4 us (97%)
  local copies, waits for them, and re-layouts  1.38 us (2%)
    pallas_call x1, Pallas kernels, on_device(): pl.pallas_call(kernel, out_shape=(jax.ShapeDtypeStruct((LOCALS, UNKNOWNS,...  63.4 us
    unnamed x2, local copies, waits for them, and re-layouts  1.38 us

profile of v3, /device:TPU:1, one launch (start us, length us, event | category | flops | bytes accessed | tf_op | source)
XLA Modules:
  0.0 65.4 jit_solution(17737767752726074234)
XLA Ops:
  0.6 63.4 %shard_map.95 = (f32[3,256,128]{2,1,0:T(8,128)S(1)}, f32[128,128]{1,0:T(8,128)S(1)}) custom-call(s32[3]{0:T(128)} %bitcast.21, f32[3,256,128]{2,1,0:T(8,128)} %bitcast.16, f32[3,256,256]{2,1,0:T(8,128)} %bitcast.15, f32[3,2,256,256]{3,2,1,0:T(8,128)} %bitcast.14, f32[128,128]{1,0:T(8,128)} %bitcast.19, f32[4,2,16,256]{3,2,1,0:T(8,128)} %bitcast.18, ...), custom_call_target="tpu_custom_call" | custom-call | tf_op jit(solution)/shard_map/pallas_call | solution.py:598
  64.0 0.7 %copy.12 = f32[1,1,3,256,128]{4,3,2,1,0:T(8,128)} copy(f32[1,1,3,256,128]{4,3,2,1,0:T(8,128)S(1)} %bitcast.12) | data formatting | bytes 786432
  64.7 0.6 copy.13

commit v4 on v3

--- a/solution.py
+++ b/solution.py
@@ -86,7 +86,7 @@
     loc_names, loc_rhs, loc_inv, loc_low, lvl_rhs, lvl_inv, lvl_low, lvl_names,
     loc_out, sol_out,
     loc_parent, lvl_parent, rhs_s, inv_s, low_s, lvl_rhs_s, inv_high, inv_rest, low_high, low_rest, y_s,
-    strips_s, snd, x_part, x_sum, y_part, y_sum, x_last, y_last, ride_snd, ride_rcv, names_snd, names_rcv,
+    strips_s, snd, x_part, x_sum, x_last, y_last, ride_snd, ride_rcv, names_snd, names_rcv,
     mats, mat_high, mat_rest, up_snd, up_rcv, down_snd, down_rcv,
     own_snd, ring_rcv, x_rcv, next_rcv, beside_rcv, sol_snd, sol_rcv, turned_s,
     load_sem, strips_sem, part_snd_sem, part_sem, last_snd_sem, last_sem,
@@ -118,6 +118,7 @@
         for slot in slots
         for there_core in cores
     ]
+    carrier_shares = [(there_y, there_core) for there_y in ys for _ in slots for there_core in cores]
     holders = [(carried, 4 * there_y + there_x) for there_y in ys for there_x in xs]
     x_carriers = [
         ((2 * z + there_core, 4 * y + x_of(core, slot)), slot, there_core)
@@ -295,24 +296,16 @@
         x_sum[...] = (x_part[0] + x_part[1]) + (x_part[2] + x_part[3])
         for device, there_y in y_others:
             send(
-                x_sum.at[there_y], x_last.at[y], last_snd_sem.at[0], last_sem.at[0], device
+                x_sum.at[there_y], x_last.at[y], last_snd_sem, last_sem, device
             ).start()
 
-    def y_first():
-        for device, there_y in y_others:
-            send(
-                snd.at[1, :, there_y], y_part.at[y], part_snd_sem.at[1], part_sem.at[1], device
-            ).start()
-
-    def y_then_x():
-        drain(y_part.at[0:3], part_sem.at[1])
-        total = snd[1, :, y]
-        for _, there_y in y_others:
-            total = total + y_part[there_y]
-        y_sum[...] = total
+    def straight():
         copies = [
-            (y_sum.at[slot, there_core], y_last.at[x], last_snd_sem.at[1], last_sem.at[1], device)
-            for device, slot, there_core in x_carriers
+            (
+                snd.at[1, slot, index_y, there_core], y_last.at[rows],
+                part_snd_sem.at[1], part_sem.at[1], device,
+            )
+            for (device, _, slot), (index_y, there_core) in zip(carriers, carrier_shares)
         ]
         for copy in copies[1:]:
             send(*copy).start()
@@ -324,7 +317,7 @@
     along_x(1)
     along_x(2)
     local_updates(1)
-    y_first()
+    straight()
     row = lax.broadcasted_iota(jnp.int32, (OCTET, 128), 0)
     names = jnp.zeros((OCTET, 128), f32)
     for k in range(2):
@@ -355,12 +348,12 @@
         inverse = (inv_high[i], inv_rest[i])
         y_s[i] = product(y_s[i], inv_high[i], inv_rest[i], 0)
         for kind in range(2):
-            high, rest = split(multiply((low_high[i, kind], low_rest[i, kind]), inverse, 0))
+            both = multiply((low_high[i, kind], low_rest[i, kind]), inverse, 0)
+            high, rest = split(both.T if kind == 0 else both)
             low_high[i, kind] = high
             low_rest[i, kind] = rest
 
     to_sibling(0)
-    y_then_x()
     drain(ride_rcv, ride_sem)
     parts = regroup(ride_rcv[...].reshape(2, 8, OCTET, 128))
     parts = [jnp.concatenate([part[0], part[1]], axis=1) for part in parts]
@@ -390,7 +383,7 @@
     below = []
     take(0)
     to_far(1)
-    drain(x_last.at[0:3], last_sem.at[0])
+    drain(x_last.at[0:3], last_sem)
     above = x_sum[y]
     for _, there_y in y_others:
         above = above + x_last[there_y]
@@ -400,13 +393,15 @@
         if level + 1 < LEVELS:
             out = [thin(moved, low_at(level, kind), 1) for kind in range(kinds)]
             if level == 0:
-                drain(y_last, last_sem.at[1])
-                pending = (y_last[0] + y_last[1]) + (y_last[2] + y_last[3])
+                drain(y_last, part_sem.at[1])
+                pending = y_last[0]
+                for source in range(1, PEERS):
+                    pending = pending + y_last[source]
             else:
                 pending = gathered(own_pending, up_rcv.at[level - 1, 1], up_sem.at[level - 1, 1])
             out[0] = out[0] + pending
             for kind in range(kinds):
-                for index in range(3):
+                for index in (1, 2, 0):
                     up_snd[level, kind, index] = chosen(parent[level], places[index], out[kind])
                     send(
                         up_snd.at[level, kind, index], up_rcv.at[level, kind, slot_at(index)],
@@ -428,7 +423,7 @@
 
     def send_down(level, kind, value):
         down_snd[level, kind] = value
-        for index in range(3):
+        for index in (1, 2, 0):
             send(
                 down_snd.at[level, kind], down_rcv.at[level, kind, slot_at(index)],
                 down_snd_sem, down_sem.at[level, kind], partners[level][index],
@@ -536,11 +531,10 @@
             else:
                 term = weight * beside_next[at_place - 2]
             grand = term if grand is None else grand + term
-        y_s[i] = y_s[i] - product(grand, low_high[i, 1], low_rest[i, 1], 0)
+        loc_out[i] = (y_s[i] - product(grand, low_high[i, 1], low_rest[i, 1], 0)).T
     drain(x_part.at[0:3], part_snd_sem.at[0])
-    drain(y_part.at[0:3], part_snd_sem.at[1])
-    drain(x_last.at[0:3], last_snd_sem.at[0])
-    drain(y_last.at[0:3], last_snd_sem.at[1])
+    drain(y_last.at[1:], part_snd_sem.at[1])
+    drain(x_last.at[0:3], last_snd_sem)
     drain(ride_rcv.at[1:], ride_snd_sem)
     drain(names_snd, names_snd_sem)
     for step in range(2):
@@ -562,7 +556,7 @@
     @pl.when(jnp.logical_not(own))
     def _():
         drain(x_part.at[0], part_snd_sem.at[0])
-        drain(y_last.at[0], last_snd_sem.at[1])
+        drain(y_last.at[0], part_snd_sem.at[1])
         drain(ride_rcv.at[0], ride_snd_sem)
         for step in range(2):
             drain(ring_rcv.at[step, 0], early_snd_sem.at[step])
@@ -574,7 +568,7 @@
     x_all = whole(x_rcv)
     for i in range(LOCALS):
         above_x = pick[i][0] * x_all[0] + pick[i][1] * x_all[1]
-        loc_out[i] = (y_s[i] - product(above_x, low_high[i, 0], low_rest[i, 0], 0)).T
+        loc_out[i] -= multiply((low_high[i, 0], low_rest[i, 0]), split(above_x), 1)
     here = pl.ds(pl.multiple_of(STRIP * rows, STRIP), STRIP)
     for k in range(2):
         turned_s[k] = x_all[k].T
@@ -619,10 +613,8 @@
             pltpu.VMEM((2, 2, 4, 2, SHARE, UNKNOWNS), f32),
             pltpu.VMEM((4, 4, SHARE, UNKNOWNS), f32),
             pltpu.VMEM((4, SHARE, UNKNOWNS), f32),
-            pltpu.VMEM((4, 2, 2, SHARE, UNKNOWNS), f32),
-            pltpu.VMEM((2, 2, SHARE, UNKNOWNS), f32),
             pltpu.VMEM((4, SHARE, UNKNOWNS), f32),
-            pltpu.VMEM((4, SHARE, UNKNOWNS), f32),
+            pltpu.VMEM((PEERS, SHARE, UNKNOWNS), f32),
             pltpu.VMEM((2, SHARES, OCTET, 128), f32),
             pltpu.VMEM((PEERS, OCTET, 128), f32),
             pltpu.VMEM((OCTET, 128), f32),
@@ -646,8 +638,8 @@
             dma((len(BLOCKS),)),
             dma((2,)),
             dma((2,)),
-            dma((2,)),
-            dma((2,)),
+            dma,
+            dma,
             dma,
             dma,
             dma,

time: 65.5 us -> 65.8 us (level)
  no operation moved by 1% of the time
where the time goes in v4:
time: 65.8 us; the launch traced here: 65.6 us
  Pallas kernels  63.6 us (97%)
  local copies, waits for them, and re-layouts  1.38 us (2%)
    pallas_call x1, Pallas kernels, on_device(): pl.pallas_call(kernel, out_shape=(jax.ShapeDtypeStruct((LOCALS, UNKNOWNS,...  63.6 us
    unnamed x2, local copies, waits for them, and re-layouts  1.38 us

profile of v4, /device:TPU:1, one launch (start us, length us, event | category | flops | bytes accessed | tf_op | source)
XLA Modules:
  0.0 65.6 jit_solution(9087431416203043129)
XLA Ops:
  0.6 63.6 %shard_map.95 = (f32[3,256,128]{2,1,0:T(8,128)S(1)}, f32[128,128]{1,0:T(8,128)S(1)}) custom-call(s32[3]{0:T(128)} %bitcast.21, f32[3,256,128]{2,1,0:T(8,128)} %bitcast.16, f32[3,256,256]{2,1,0:T(8,128)} %bitcast.15, f32[3,2,256,256]{3,2,1,0:T(8,128)} %bitcast.14, f32[128,128]{1,0:T(8,128)} %bitcast.19, f32[4,2,16,256]{3,2,1,0:T(8,128)} %bitcast.18, ...), custom_call_target="tpu_custom_call" | custom-call | tf_op jit(solution)/shard_map/pallas_call | solution.py:592
  64.3 0.7 %copy.12 = f32[1,1,3,256,128]{4,3,2,1,0:T(8,128)} copy(f32[1,1,3,256,128]{4,3,2,1,0:T(8,128)S(1)} %bitcast.12) | data formatting | bytes 786432
  65.0 0.6 copy.13

commit v5 on v4

--- a/solution.py
+++ b/solution.py
@@ -85,9 +85,9 @@
 def kernel(
     loc_names, loc_rhs, loc_inv, loc_low, lvl_rhs, lvl_inv, lvl_low, lvl_names,
     loc_out, sol_out,
-    loc_parent, lvl_parent, rhs_s, inv_s, low_s, lvl_rhs_s, inv_high, inv_rest, low_high, low_rest, y_s,
+    loc_parent, lvl_parent, rhs_s, inv_s, low_s, lvl_rhs_s, inv_high, inv_rest, low_high, low_rest, y_s, solved_s, sums_s,
     strips_s, snd, x_part, x_sum, x_last, y_last, ride_snd, ride_rcv, names_snd, names_rcv,
-    mats, mat_high, mat_rest, up_snd, up_rcv, down_snd, down_rcv,
+    mats, mat_high, mat_rest, turned_high, turned_rest, up_snd, up_rcv, down_snd, down_rcv,
     own_snd, ring_rcv, x_rcv, next_rcv, beside_rcv, sol_snd, sol_rcv, turned_s,
     load_sem, strips_sem, part_snd_sem, part_sem, last_snd_sem, last_sem,
     ride_snd_sem, ride_sem, names_snd_sem, names_sem, strip_snd_sem, strip_sem, ring_snd_sem, ring_sem, far_sem,
@@ -182,7 +182,7 @@
         high, rest = split(inv_s[i])
         inv_high[i] = high
         inv_rest[i] = rest
-        y_s[i] = product(rhs_s[i].T, high, rest, 1)
+        solved_s[i] = multiply((high, rest), split(rhs_s[i]), 0)
     pl.semaphore_wait(barrier, len(others) + jnp.where(own, 0, 2))
 
     def send(src, dst, send_sem, recv_sem, device):
@@ -250,10 +250,18 @@
         for m in range(3 * index, 3 * index + 3):
             name, level = BLOCKS[m][:2]
             if name == "low":
-                mat_high[m], mat_rest[m] = split(multiply(parts[BLOCKS[m]], parts["inv", level], 0))
+                both = multiply(parts[BLOCKS[m]], parts["inv", level], 0)
+                mat_high[m], mat_rest[m] = split(both)
+                if index > 0:
+                    turned_high[m], turned_rest[m] = split(both.T)
             elif level + 1 == LEVELS:
                 turned = split(mats[m].reshape(UNKNOWNS, UNKNOWNS).T)
                 mat_high[m], mat_rest[m] = split(multiply(turned, parts[BLOCKS[m]], 0))
+
+    def thin_up(vectors, m):
+        if m < 3:
+            return thin(vectors, m, 1)
+        return thin_product(vectors, turned_high[m], turned_rest[m], 0)
 
     def thin(vectors, m, dim):
         return thin_product(vectors, mat_high[m], mat_rest[m], dim)
@@ -275,12 +283,14 @@
             high, rest = split(low_s[i, kind])
             low_high[i, kind] = high
             low_rest[i, kind] = rest
-            update = product(y_s[i], high, rest, 1).reshape(4, 2, SHARE, UNKNOWNS)
+            update = multiply((high, rest), split(solved_s[i]), 0)
             for slot in range(2):
                 if i == 0:
-                    snd[kind, slot] = pick[i][slot] * update
+                    sums_s[slot] = pick[i][slot] * update
                 else:
-                    snd[kind, slot] += pick[i][slot] * update
+                    sums_s[slot] += pick[i][slot] * update
+        for slot in range(2):
+            snd[kind, slot] = sums_s[slot].T.reshape(4, 2, SHARE, UNKNOWNS)
 
     def x_first():
         copies = [
@@ -346,7 +356,7 @@
 
     def prepare_local(i):
         inverse = (inv_high[i], inv_rest[i])
-        y_s[i] = product(y_s[i], inv_high[i], inv_rest[i], 0)
+        y_s[i] = product(solved_s[i].T, inv_high[i], inv_rest[i], 0)
         for kind in range(2):
             both = multiply((low_high[i, kind], low_rest[i, kind]), inverse, 0)
             high, rest = split(both.T if kind == 0 else both)
@@ -391,7 +401,7 @@
         kinds = kinds_at(level)
         moved = rhs[level] - above
         if level + 1 < LEVELS:
-            out = [thin(moved, low_at(level, kind), 1) for kind in range(kinds)]
+            out = [thin_up(moved, low_at(level, kind)) for kind in range(kinds)]
             if level == 0:
                 drain(y_last, part_sem.at[1])
                 pending = y_last[0]
@@ -609,6 +619,8 @@
             pltpu.VMEM((LOCALS, 2) + square, bf16),
             pltpu.VMEM((LOCALS, 2) + square, bf16),
             pltpu.VMEM((LOCALS, COLUMNS, UNKNOWNS), f32),
+            pltpu.VMEM((LOCALS, UNKNOWNS, COLUMNS), f32),
+            pltpu.VMEM((2, UNKNOWNS, COLUMNS), f32),
             pltpu.VMEM((2, len(BLOCKS), STRIP, UNKNOWNS), f32),
             pltpu.VMEM((2, 2, 4, 2, SHARE, UNKNOWNS), f32),
             pltpu.VMEM((4, 4, SHARE, UNKNOWNS), f32),
@@ -620,6 +632,8 @@
             pltpu.VMEM((OCTET, 128), f32),
             pltpu.VMEM((OCTET, 128), f32),
             pltpu.VMEM((len(BLOCKS), 4, 2, 2 * STRIP, UNKNOWNS), f32),
+            pltpu.VMEM((len(BLOCKS),) + square, bf16),
+            pltpu.VMEM((len(BLOCKS),) + square, bf16),
             pltpu.VMEM((len(BLOCKS),) + square, bf16),
             pltpu.VMEM((len(BLOCKS),) + square, bf16),
             pltpu.VMEM((LEVELS - 1, 2, 3, SHARE, UNKNOWNS), f32),

time: 65.8 us -> 65.4 us (level)
  no operation moved by 1% of the time
where the time goes in v5:
time: 65.4 us; the launch traced here: 65.3 us
  Pallas kernels  63.2 us (97%)
  local copies, waits for them, and re-layouts  1.38 us (2%)
    pallas_call x1, Pallas kernels, on_device(): pl.pallas_call(kernel, out_shape=(jax.ShapeDtypeStruct((LOCALS, UNKNOWNS,...  63.2 us
    unnamed x2, local copies, waits for them, and re-layouts  1.38 us

profile of v5, /device:TPU:1, one launch (start us, length us, event | category | flops | bytes accessed | tf_op | source)
XLA Modules:
  0.0 65.3 jit_solution(12209110488679046085)
XLA Ops:
  0.6 63.2 %shard_map.95 = (f32[3,256,128]{2,1,0:T(8,128)S(1)}, f32[128,128]{1,0:T(8,128)S(1)}) custom-call(s32[3]{0:T(128)} %bitcast.21, f32[3,256,128]{2,1,0:T(8,128)} %bitcast.16, f32[3,256,256]{2,1,0:T(8,128)} %bitcast.15, f32[3,2,256,256]{3,2,1,0:T(8,128)} %bitcast.14, f32[128,128]{1,0:T(8,128)} %bitcast.19, f32[4,2,16,256]{3,2,1,0:T(8,128)} %bitcast.18, ...), custom_call_target="tpu_custom_call" | custom-call | tf_op jit(solution)/shard_map/pallas_call | solution.py:602
  63.9 0.7 %copy.12 = f32[1,1,3,256,128]{4,3,2,1,0:T(8,128)} copy(f32[1,1,3,256,128]{4,3,2,1,0:T(8,128)S(1)} %bitcast.12) | data formatting | bytes 786432
  64.6 0.6 copy.13

commit v6 on v5

--- a/solution.py
+++ b/solution.py
@@ -80,6 +80,19 @@
 
 def trio(index):
     return slice(3 * index, 3 * index + 3)
+
+
+def pieces(index, upper):
+    if not upper:
+        return [(trio(index), slice(0, UNKNOWNS))]
+    found = []
+    for m in range(3 * index, 3 * index + 3):
+        lanes = slice(0, HALF if BLOCKS[m][0] == "inv" else UNKNOWNS)
+        if found and found[-1][1] == lanes:
+            found[-1] = (slice(found[-1][0].start, m + 1), lanes)
+        else:
+            found.append((slice(m, m + 1), lanes))
+    return found
 
 
 def kernel(
@@ -161,6 +174,9 @@
     for load in loads + strip_loads:
         load.start()
 
+    for level in range(LEVELS):
+        mats[inv_at(level), 0:2, :, :, HALF:] = jnp.zeros((2, 2, 2 * STRIP, HALF), f32)
+
     barrier = pltpu.get_barrier_semaphore()
 
     def greet(device):
@@ -208,40 +224,86 @@
     strip = pl.ds(pl.multiple_of(STRIP * parity, STRIP), STRIP)
     first, second = slice(0, STRIP), slice(STRIP, 2 * STRIP)
 
+    def by_rows(at_y, index, act):
+        for upper in (True, False):
+
+            @pl.when((at_y < 2) if upper else (at_y >= 2))
+            def _():
+                for blocks, lanes in pieces(index, upper):
+                    act(blocks, lanes)
+
     def along_x(index):
-        copies = [
-            (
-                strips_s.at[slot, trio(index)], mats.at[trio(index), y, x_high, strip, :],
-                strip_snd_sem, strip_sem.at[index], (2 * z + x_high, 4 * y + x_of(core, slot)),
-            )
-            for slot in slots
-        ]
-        send(*copies[1]).start()
-        send_or_keep(copies[:1])
+        def start(blocks, lanes):
+            copies = [
+                (
+                    strips_s.at[slot, blocks, :, lanes],
+                    mats.at[blocks, y, x_high, strip, lanes],
+                    strip_snd_sem, strip_sem.at[index], (2 * z + x_high, 4 * y + x_of(core, slot)),
+                )
+                for slot in slots
+            ]
+            send(*copies[1]).start()
+            send_or_keep(copies[:1])
+
+        by_rows(y, index, start)
+
+    def rows_of(at_y, part):
+        return lambda blocks, lanes: mats.at[blocks, at_y, core, part, lanes]
+
+    def wait_rows(at_y, index, part, sem):
+        by_rows(at_y, index, lambda blocks, lanes: drain(rows_of(at_y, part)(blocks, lanes), sem))
+
+    def units(index, upper):
+        return sum(
+            (blocks.stop - blocks.start) * (lanes.stop // HALF) for blocks, lanes in pieces(index, upper)
+        )
+
+    def wait_all(at_y, index, sem):
+        for upper in (True, False):
+
+            @pl.when((at_y < 2) if upper else (at_y >= 2))
+            def _():
+                drain(y_last.at[0 : units(index, upper)], sem)
+
+    def send_rows(at_y, index, part, sem, device):
+        def start(blocks, lanes):
+            ref = rows_of(at_y, part)(blocks, lanes)
+            send(ref, ref, ring_snd_sem, sem, device).start()
+
+        by_rows(at_y, index, start)
+
+    every = slice(0, 2 * STRIP)
 
     def along_y(index):
-        part = mats.at[trio(index), y, core]
-        drain(part, strip_sem.at[index])
+        wait_all(y, index, strip_sem.at[index])
         for device in (up, down):
-            send(part, part, ring_snd_sem, ring_sem.at[index], device).start()
+            send_rows(y, index, every, ring_sem.at[index], device)
         if index == 0:
-            send(part, part, ring_snd_sem, far_sem.at[index], far).start()
+            send_rows(y, index, every, far_sem.at[index], far)
+
+    def wait_ring(index):
+        drain(y_last.at[0 : units(index, True) + units(index, False)], ring_sem.at[index])
 
     def to_far(index):
-        drain(mats.at[trio(index), 0:2, core], ring_sem.at[index])
+        wait_ring(index)
         for at_y, half_strip, device in ((y_down, first, up), (y_up, second, down)):
-            part = mats.at[trio(index), at_y, core, half_strip, :]
-            send(part, part, ring_snd_sem, far_sem.at[index], device).start()
+            send_rows(at_y, index, half_strip, far_sem.at[index], device)
+
+    def pair_parts(index, collector):
+        return [
+            mats.at[blocks, 0:2, collector, :, lanes] for blocks, lanes in pieces(index, True)
+        ] + [mats.at[trio(index), 2:4, collector]]
 
     def to_sibling(index):
         if index == 0:
-            drain(mats.at[trio(index), 0:2, core], ring_sem.at[index])
-        drain(mats.at[trio(index), y_far, core], far_sem.at[index])
-        part = mats.at[trio(index), :, core]
-        send(part, part, pair_snd_sem, pair_sem.at[index], sibling).start()
+            wait_ring(index)
+        wait_all(y_far, index, far_sem.at[index])
+        for n, part in enumerate(pair_parts(index, core)):
+            send(part, part, pair_snd_sem, pair_sem.at[index, n], sibling).start()
 
     def take(index):
-        drain(mats.at[trio(index), :, 1 - core], pair_sem.at[index])
+        for n, part in enumerate(pair_parts(index, 1 - core)):
+            drain(part, pair_sem.at[index, n])
         parts = {}
         for m in range(3 * index, 3 * index + 3):
             parts[BLOCKS[m]] = split(mats[m].reshape(UNKNOWNS, UNKNOWNS))
@@ -554,9 +616,22 @@
             drain(ring_rcv.at[step], late_snd_sem.at[step, 0])
         drain(x_rcv.at[:, 0:3, :, 1], late_snd_sem.at[step, 1])
     drain(sol_snd.at[1:], sol_snd_sem)
-    drain(strips_s.at[0], strip_snd_sem)
-    drain(mats.at[:, 0:3, 0], ring_snd_sem)
-    drain(mats.at[:, :, 0], pair_snd_sem)
+    def strips_sent():
+        for index in range(TRIOS):
+            by_rows(
+                y, index,
+                lambda blocks, lanes: drain(strips_s.at[0, blocks, :, lanes], strip_snd_sem),
+            )
+
+    strips_sent()
+    for index in range(TRIOS):
+        for _ in range(3 if index == 0 else 2):
+            wait_rows(y, index, every, ring_snd_sem)
+        if index > 0:
+            wait_rows(y_down, index, first, ring_snd_sem)
+            wait_rows(y_up, index, second, ring_snd_sem)
+        for part in pair_parts(index, core):
+            drain(part, pair_snd_sem)
     drain(beside_rcv, beside_snd_sem)
     for level in range(LEVELS - 1):
         for kind in range(kinds_at(level)):
@@ -572,7 +647,7 @@
             drain(ring_rcv.at[step, 0], early_snd_sem.at[step])
             drain(ring_rcv.at[step], late_snd_sem.at[step, 0])
         drain(sol_snd.at[0], sol_snd_sem)
-        drain(strips_s.at[0], strip_snd_sem)
+        strips_sent()
 
     spread_end(1, x_rcv)
     x_all = whole(x_rcv)
@@ -664,7 +739,7 @@
             dma((TRIOS,)),
             dma((TRIOS,)),
             dma,
-            dma((TRIOS,)),
+            dma((TRIOS, 4)),
             dma,
             dma((LEVELS - 1, 2)),
             dma,

time: 65.4 us -> 65.5 us (level)
  no operation moved by 1% of the time
where the time goes in v6:
time: 65.5 us; the launch traced here: 65.4 us
  Pallas kernels  63.3 us (97%)
  local copies, waits for them, and re-layouts  1.38 us (2%)
    pallas_call x1, Pallas kernels, on_device(): pl.pallas_call(kernel, out_shape=(jax.ShapeDtypeStruct((LOCALS, UNKNOWNS,...  63.3 us
    unnamed x2, local copies, waits for them, and re-layouts  1.38 us

profile of v6, /device:TPU:1, one launch (start us, length us, event | category | flops | bytes accessed | tf_op | source)
XLA Modules:
  0.0 65.4 jit_solution(11851096410605901769)
XLA Ops:
  0.6 63.3 %shard_map.95 = (f32[3,256,128]{2,1,0:T(8,128)S(1)}, f32[128,128]{1,0:T(8,128)S(1)}) custom-call(s32[3]{0:T(128)} %bitcast.21, f32[3,256,128]{2,1,0:T(8,128)} %bitcast.16, f32[3,256,256]{2,1,0:T(8,128)} %bitcast.15, f32[3,2,256,256]{3,2,1,0:T(8,128)} %bitcast.14, f32[128,128]{1,0:T(8,128)} %bitcast.19, f32[4,2,16,256]{3,2,1,0:T(8,128)} %bitcast.18, ...), custom_call_target="tpu_custom_call" | custom-call | tf_op jit(solution)/shard_map/pallas_call | solution.py:677
  64.0 0.7 %copy.12 = f32[1,1,3,256,128]{4,3,2,1,0:T(8,128)} copy(f32[1,1,3,256,128]{4,3,2,1,0:T(8,128)S(1)} %bitcast.12) | data formatting | bytes 786432
  64.7 0.6 copy.13

commit v7 on v5

--- a/solution.py
+++ b/solution.py
@@ -87,7 +87,7 @@
     loc_out, sol_out,
     loc_parent, lvl_parent, rhs_s, inv_s, low_s, lvl_rhs_s, inv_high, inv_rest, low_high, low_rest, y_s, solved_s, sums_s,
     strips_s, snd, x_part, x_sum, x_last, y_last, ride_snd, ride_rcv, names_snd, names_rcv,
-    mats, mat_high, mat_rest, turned_high, turned_rest, up_snd, up_rcv, down_snd, down_rcv,
+    mats, mat_high, mat_rest, up_snd, up_rcv, down_snd, down_rcv,
     own_snd, ring_rcv, x_rcv, next_rcv, beside_rcv, sol_snd, sol_rcv, turned_s,
     load_sem, strips_sem, part_snd_sem, part_sem, last_snd_sem, last_sem,
     ride_snd_sem, ride_sem, names_snd_sem, names_sem, strip_snd_sem, strip_sem, ring_snd_sem, ring_sem, far_sem,
@@ -252,16 +252,9 @@
             if name == "low":
                 both = multiply(parts[BLOCKS[m]], parts["inv", level], 0)
                 mat_high[m], mat_rest[m] = split(both)
-                if index > 0:
-                    turned_high[m], turned_rest[m] = split(both.T)
             elif level + 1 == LEVELS:
                 turned = split(mats[m].reshape(UNKNOWNS, UNKNOWNS).T)
                 mat_high[m], mat_rest[m] = split(multiply(turned, parts[BLOCKS[m]], 0))
-
-    def thin_up(vectors, m):
-        if m < 3:
-            return thin(vectors, m, 1)
-        return thin_product(vectors, turned_high[m], turned_rest[m], 0)
 
     def thin(vectors, m, dim):
         return thin_product(vectors, mat_high[m], mat_rest[m], dim)
@@ -390,6 +383,7 @@
             total = total + buffer[index]
         return total
 
+    sums = []
     below = []
     take(0)
     to_far(1)
@@ -401,7 +395,7 @@
         kinds = kinds_at(level)
         moved = rhs[level] - above
         if level + 1 < LEVELS:
-            out = [thin_up(moved, low_at(level, kind)) for kind in range(kinds)]
+            out = [thin(moved, low_at(level, kind), 1) for kind in range(kinds)]
             if level == 0:
                 drain(y_last, part_sem.at[1])
                 pending = y_last[0]
@@ -421,11 +415,12 @@
             if level == 0:
                 to_sibling(1)
                 to_far(2)
-            below.append(thin(thin(moved, inv_at(level), 1), inv_at(level), 0))
+            sums.append(moved)
             if level + 1 < TRIOS:
                 take(level + 1)
             else:
-                prepare_local(0)
+                for index, value in enumerate(sums):
+                    below.append(thin(thin(value, inv_at(index), 1), inv_at(index), 0))
             if level == 0:
                 to_sibling(2)
             own_above = chosen(parent[level], mine, out[0])
@@ -496,9 +491,9 @@
         send_down(level, 0, current)
         if level == 0:
             spread(0, next_rcv, current)
+        prepare_local(LEVELS - 2 - level)
+        if level == 0:
             spread_on(0, next_rcv)
-        else:
-            prepare_local(LEVELS - 1 - level)
         left = below[level]
         if kinds_at(level) == 2:
             left = left - thin(pooled(level, 1, current_parent), low_at(level, 1), 0)
@@ -634,8 +629,6 @@
             pltpu.VMEM((len(BLOCKS), 4, 2, 2 * STRIP, UNKNOWNS), f32),
             pltpu.VMEM((len(BLOCKS),) + square, bf16),
             pltpu.VMEM((len(BLOCKS),) + square, bf16),
-            pltpu.VMEM((len(BLOCKS),) + square, bf16),
-            pltpu.VMEM((len(BLOCKS),) + square, bf16),
             pltpu.VMEM((LEVELS - 1, 2, 3, SHARE, UNKNOWNS), f32),
             pltpu.VMEM((LEVELS - 1, 2, 3, SHARE, UNKNOWNS), f32),
             pltpu.VMEM((LEVELS - 1, 2, SHARE, UNKNOWNS), f32),

time: 65.4 us -> 65.8 us (level)
  no operation moved by 1% of the time
where the time goes in v7:
time: 65.8 us; the launch traced here: 65.7 us
  Pallas kernels  63.6 us (97%)
  local copies, waits for them, and re-layouts  1.38 us (2%)
    pallas_call x1, Pallas kernels, on_device(): pl.pallas_call(kernel, out_shape=(jax.ShapeDtypeStruct((LOCALS, UNKNOWNS,...  63.6 us
    unnamed x2, local copies, waits for them, and re-layouts  1.38 us

profile of v7, /device:TPU:1, one launch (start us, length us, event | category | flops | bytes accessed | tf_op | source)
XLA Modules:
  0.0 65.7 jit_solution(5540606498745769354)
XLA Ops:
  0.6 63.6 %shard_map.95 = (f32[3,256,128]{2,1,0:T(8,128)S(1)}, f32[128,128]{1,0:T(8,128)S(1)}) custom-call(s32[3]{0:T(128)} %bitcast.21, f32[3,256,128]{2,1,0:T(8,128)} %bitcast.16, f32[3,256,256]{2,1,0:T(8,128)} %bitcast.15, f32[3,2,256,256]{3,2,1,0:T(8,128)} %bitcast.14, f32[128,128]{1,0:T(8,128)} %bitcast.19, f32[4,2,16,256]{3,2,1,0:T(8,128)} %bitcast.18, ...), custom_call_target="tpu_custom_call" | custom-call | tf_op jit(solution)/shard_map/pallas_call | solution.py:597
  64.3 0.7 %copy.12 = f32[1,1,3,256,128]{4,3,2,1,0:T(8,128)} copy(f32[1,1,3,256,128]{4,3,2,1,0:T(8,128)S(1)} %bitcast.12) | data formatting | bytes 786432
  65.0 0.6 copy.13
